TPU v7x, 128 devices: a whole 4x4x4 slice. The times are simulated.
128 devices in a mesh: lat: 4 (over y_hi, core), lon: 32 (over x, z, y_lo).
Axes of the slice: x: 4, y: 4 (y_hi: 2, y_lo: 2; y = y_hi * 2 + y_lo), z: 4, core: 2. Of those that a mesh axis runs over, the one named last changes fastest.
Arguments:
- tokens: bfloat16 [256, 2048, 256], P('lat', 'lon'), may hold values from -6 to 6
- gain_conv: float32 [256], replicated, may hold values from 0.25 to 1.75
- w_expand: bfloat16 [256, 1024], replicated, may hold values from -0.375 to 0.375
- dw_kernel: float32 [3, 3, 1024], replicated, may hold values from -2 to 2
- w_project: bfloat16 [1024, 256], replicated, may hold values from -0.1875 to 0.1875
- gain_block: float32 [256], replicated, may hold values from 0.25 to 1.75
- qkv_block: bfloat16 [256, 768], replicated, may hold values from -0.375 to 0.375
- bias_block: float32 [8, 64, 64], replicated, may hold values from -8 to 310
- out_block: bfloat16 [256, 256], replicated, may hold values from -0.375 to 0.375
- gain_grid: float32 [256], replicated, may hold values from 0.25 to 1.75
- qkv_grid: bfloat16 [256, 768], replicated, may hold values from -0.375 to 0.375
- bias_grid: float32 [8, 64, 64], replicated, may hold values from -8 to 310
- out_grid: bfloat16 [256, 256], replicated, may hold values from -0.375 to 0.375
Outputs:
- layer_out: bfloat16 [256, 2048, 256], P('lat', 'lon')
All inputs are finite; a program needn't handle non-finite values.
Results may differ from a plain program's by a relative error of at most 0.011.
Values may be sent and summed in bfloat16 or wider, within the bound.
A program may use at most 128 MiB of HBM per device.

v0:
```python
import jax
import jax.numpy as jnp
from jax import lax
from jax.sharding import PartitionSpec as P


def padded_2(block, sides, width, periodic):
    for axis, dim in sides:
        count = lax.axis_size(axis)
        forward = [(i, i + 1) for i in range(count - 1)]
        if periodic:
            forward.append((count - 1, 0))
        backward = [(target, source) for source, target in forward]
        low = lax.ppermute(
            lax.slice_in_dim(block, block.shape[dim] - width, None, axis=dim), axis, forward
        )
        high = lax.ppermute(lax.slice_in_dim(block, 0, width, axis=dim), axis, backward)
        block = jnp.concatenate([low, block, high], axis=dim)
    return block


def layer_norm(x, gain):
    xf = x.astype(jnp.float32)
    mean = jnp.mean(xf, axis=-1, keepdims=True)
    var = jnp.mean((xf - mean) ** 2, axis=-1, keepdims=True)
    return (xf - mean) / jnp.sqrt(var + 1e-05) * gain


def expand_tokens(x, gain, w_expand):
    normed = layer_norm(x, gain).astype(jnp.bfloat16)
    return jax.nn.gelu(jnp.dot(normed, w_expand, preferred_element_type=jnp.float32)).astype(
        jnp.bfloat16
    )


def attend(x, gain, w_qkv, bias, w_out):
    groups = x.shape[0]
    width = x.shape[2]
    heads = bias.shape[0]
    head_size = width // heads
    normed = layer_norm(x, gain).astype(jnp.bfloat16)
    qkv = jnp.dot(normed.reshape(-1, width), w_qkv, preferred_element_type=jnp.float32).astype(
        jnp.bfloat16
    )
    qkv = qkv.reshape(groups, 64, 3, heads, head_size)
    scores = jnp.einsum(
        "gqhe,gkhe->ghqk", qkv[:, :, 0], qkv[:, :, 1], preferred_element_type=jnp.float32
    )
    scores = scores * head_size ** (-0.5) + bias[None]
    scores = scores - jnp.max(scores, axis=-1, keepdims=True)
    expo = jnp.exp(scores)
    weights = (expo / jnp.sum(expo, axis=-1, keepdims=True)).astype(jnp.bfloat16)
    mixed = jnp.einsum(
        "ghqk,gkhe->gqhe", weights, qkv[:, :, 2], preferred_element_type=jnp.float32
    ).astype(jnp.bfloat16)
    result = jnp.dot(mixed.reshape(-1, width), w_out, preferred_element_type=jnp.float32)
    return result.reshape(groups, 64, width)


def shards(
    tokens,
    gain_conv,
    w_expand,
    dw_kernel,
    w_project,
    gain_block,
    qkv_block,
    bias_block,
    out_block,
    gain_grid,
    qkv_grid,
    bias_grid,
    out_grid,
):
    rows, cols, width = tokens.shape
    lat_count = lax.axis_size("lat")
    lon_count = lax.axis_size("lon")
    expanded = expand_tokens(tokens, gain_conv, w_expand)
    padded = padded_2(expanded, (("lat", 0),), 1, False)
    padded = padded_2(padded, (("lon", 1),), 1, True)
    total = jnp.zeros((rows, cols, padded.shape[2]), jnp.float32)
    for row_step in range(3):
        for col_step in range(3):
            total = (
                total
                + padded[row_step : row_step + rows, col_step : col_step + cols].astype(jnp.float32)
                * dw_kernel[row_step, col_step]
            )
    conv = jax.nn.gelu(total).astype(jnp.bfloat16)
    mixed = (
        tokens.astype(jnp.float32) + jnp.dot(conv, w_project, preferred_element_type=jnp.float32)
    ).astype(jnp.bfloat16)
    blocks = (
        mixed.reshape(rows // 8, 8, cols // 8, 8, width)
        .transpose(0, 2, 1, 3, 4)
        .reshape(-1, 64, width)
    )
    block_out = attend(blocks, gain_block, qkv_block, bias_block, out_block)
    blocked = (blocks.astype(jnp.float32) + block_out).astype(jnp.bfloat16)
    blocked = (
        blocked.reshape(rows // 8, cols // 8, 8, 8, width)
        .transpose(0, 2, 1, 3, 4)
        .reshape(rows, cols, width)
    )
    per_lat = 8 // lat_count
    lat_piece = rows // 8
    lon_piece = cols // lon_count
    lon_groups = lon_count // 8
    layout = blocked.reshape(per_lat, lat_count, lat_piece, lon_count, lon_piece, width)
    flat = layout.transpose(0, 1, 3, 2, 4, 5).reshape(
        per_lat, lat_count * lon_count, lat_piece, lon_piece, width
    )
    moved = lax.all_to_all(flat, ("lat", "lon"), split_axis=1, concat_axis=1, tiled=True)
    moved = moved.reshape(per_lat, lat_count, lon_count, lat_piece, lon_piece, width).transpose(
        1, 0, 3, 2, 4, 5
    )
    arranged = moved.reshape(8, lat_piece, 8, lon_groups, lon_piece, width)
    groups = arranged.transpose(1, 3, 4, 0, 2, 5).reshape(-1, 64, width)
    grid_out = attend(groups, gain_grid, qkv_grid, bias_grid, out_grid)
    finished = (groups.astype(jnp.float32) + grid_out).astype(jnp.bfloat16)
    finished = finished.reshape(lat_piece, lon_groups, lon_piece, 8, 8, width).transpose(
        3, 0, 4, 1, 2, 5
    )
    outgoing = finished.reshape(
        lat_count, per_lat, lat_piece, lon_count, lon_piece, width
    ).transpose(1, 0, 3, 2, 4, 5)
    outgoing = outgoing.reshape(per_lat, lat_count * lon_count, lat_piece, lon_piece, width)
    returned = lax.all_to_all(outgoing, ("lat", "lon"), split_axis=1, concat_axis=1, tiled=True)
    returned = returned.reshape(
        per_lat, lat_count, lon_count, lat_piece, lon_piece, width
    ).transpose(0, 1, 3, 2, 4, 5)
    return returned.reshape(rows, cols, width)


def solution(mesh):
    placed = (P("lat", "lon", None), P(), P(), P(), P(), P(), P(), P(), P(), P(), P(), P(), P())
    return jax.shard_map(
        shards, mesh=mesh, in_specs=placed, out_specs=P("lat", "lon", None), check_vma=False
    )
```

profile of v0, /device:TPU:1, one launch (start us, length us, event | category | flops | bytes accessed | tf_op | source)
XLA Modules:
  0.0 406.2 jit_solution(10235870520093653286)
XLA Ops:
  4.9 7.8 %fusion.9 = bf16[64,64,1024]{2,1,0:T(8,128)(2,1)S(1)} fusion(bf16[64,64,256]{2,1,0:T(8,128)(2,1)} %param.13, f32[256]{0:T(256)} %param.14, f32[64,64]{1,0:T(8,128)S(1)} %add_sqrt_fusion.2, f32[64,64]{1,0:T(8,128)S(1)} %broadcast_multiply_fusion.2, bf16[256,1024]{1,0:T(8,128)(2,1)S(1)} %copy-done), kind=kOutput, calls=%fused_computation.11 | convolution fusion | flops 2190475264 | bytes 11043840 | tf_op jit(solution)/shard_map/dot_general | solution.py:31
  12.7 3.2 copy-done.3
  15.9 6.2 %collective-permute-start = (bf16[1,64,1024]{2,1,0:T(8,128)(2,1)S(1)}, bf16[1,64,1024]{2,1,0:T(8,128)(2,1)S(1)}, u32[]{:S(2)}, u32[]{:S(2)}) collective-permute-start(bf16[1,64,1024]{2,1,0:T(8,128)(2,1)S(1)} %get-tuple-element.15), channel_id=1, source_target_pairs={{0,32},{32,64},{64,96},{1,33},{33,65},{65,97},{2,34},{34,66},{66,9... | collective-permute-start | bytes 393224 | tf_op jit(solution)/shard_map/ppermute | solution.py:14
  24.2 6.1 %collective-permute-done.1 = bf16[1,64,1024]{2,1,0:T(8,128)(2,1)S(1)} collective-permute-done((bf16[1,64,1024]{2,1,0:T(8,128)(2,1)S(1)}, bf16[1,64,1024]{2,1,0:T(8,128)(2,1)S(1)}, u32[]{:S(2)}, u32[]{:S(2)}) %collective-permute-start.1) | collective-permute-done | bytes 131104 | tf_op jit(solution)/shard_map/ppermute | solution.py:17
  32.4 9.8 %collective-permute-start.3 = (bf16[66,1,1024]{2,1,0:T(2,128)(2,1)S(1)}, bf16[66,1,1024]{2,1,0:T(2,128)(2,1)S(1)}, u32[]{:S(2)}, u32[]{:S(2)}) collective-permute-start(bf16[66,1,1024]{2,1,0:T(2,128)(2,1)S(1)} %get-tuple-element.14), channel_id=1, source_target_pairs={{1,0},{2,1},{3,2},{4,3},{5,4},{6,5},{7,6},{8,7},{9,8},{10,9},{11,1... | collective-permute-start | bytes 405512 | tf_op jit(solution)/shard_map/ppermute | solution.py:17
  42.2 3.6 collective-permute-done.2
  45.9 13.8 %maximum_maximum_fusion = (bf16[66,65,1024]{2,1,0:T(8,128)(2,1)}, bf16[66,65,1024]{2,1,0:T(8,128)(2,1)}) fusion(bf16[1,64,1024]{2,1,0:T(8,128)(2,1)S(1)} %collective-permute-done.1, bf16[64,64,1024]{2,1,0:T(8,128)(2,1)S(1)} %copy-done.4, bf16[1,64,1024]{2,1,0:T(8,128)(2,1)S(1)} %collective-permute-done, bf16[66,1,1024]{2,1,0:T(2,128)(2,1)S(1)} %collective-permute-done.2, ...), kind=kLoop, calls=%fused_computation.28 | loop fusion | flops 70287360 | bytes 26492928 | tf_op jit(solution)/shard_map/concatenate | solution.py:18
  59.7 32.1 %fusion.33 = bf16[64,64,256]{2,1,0:T(8,128)(2,1)} fusion(bf16[64,64,256]{2,1,0:T(8,128)(2,1)} %param.13, bf16[64,64,1024]{2,1,0:T(8,128)(2,1)S(1)} %copy-done.4, bf16[66,65,1024]{2,1,0:T(8,128)(2,1)} %get-tuple-element.12, bf16[1,64,1024]{2,1,0:T(8,128)(2,1)S(1)} %collective-permute-done.1, bf16[66,65,1024]{2,1,0:T(8,128)(2,1)} %get-tuple-element.11, ...), kind=kOutput, calls=%fused_computation.49 | convolution fusion | flops 2305818624 | bytes 63737856 | tf_op jit(solution)/shard_map/dot_general | solution.py:91
  94.2 4.2 %copy.127 = f32[8,8,8,8,256]{4,3,1,2,0:T(8,128)} copy(bf16[8,8,8,8,256]{4,3,2,1,0:T(8,128)(2,1)} %bitcast.128) | data formatting | bytes 6291456 | tf_op jit(solution)/shard_map/convert_element_type | solution.py:99
  100.2 4.6 %fusion.38 = bf16[4096,256]{1,0:T(8,128)(2,1)S(1)} fusion(f32[8,8,8,8,256]{4,3,1,2,0:T(8,128)} %copy.127, f32[256]{0:T(256)S(1)} %copy-done.13, f32[4096]{0:T(1024)S(1)} %sqrt.32, f32[4096]{0:T(1024)S(1)} %div.69), kind=kLoop, calls=%fused_computation.62 | loop fusion | flops 4194304 | bytes 6325248 | tf_op jit(solution)/shard_map/convert_element_type | solution.py:41
  104.8 4.5 %convolution_convert_fusion.1 = bf16[4096,768]{1,0:T(8,128)(2,1)} fusion(bf16[4096,256]{1,0:T(8,128)(2,1)S(1)} %fusion.38, bf16[256,768]{1,0:T(8,128)(2,1)S(1)} %copy-done.6), kind=kOutput, calls=%fused_computation.40 | convolution fusion | flops 1613758464 | bytes 8781824 | tf_op jit(solution)/shard_map/dot_general | solution.py:42
  109.3 8.6 %copy.128 = bf16[4096,768]{0,1:T(8,128)(2,1)} copy(bf16[4096,768]{1,0:T(8,128)(2,1)} %convolution_convert_fusion.1) | data formatting | bytes 12582912 | tf_op jit(solution)/shard_map/convert_element_type | solution.py:42
  117.9 17.9 %reshape.153 = bf16[64,64,3,8,32]{1,0,4,3,2:T(8,128)(2,1)} reshape(bf16[4096,768]{0,1:T(8,128)(2,1)} %copy.128) | data formatting | bytes 12582912 | tf_op jit(solution)/shard_map/reshape | solution.py:45
  135.8 7.9 %fusion.64 = (bf16[64,64,1,8,32]{1,0,4,3,2:T(8,128)(2,1)}, bf16[64,64,1,8,32]{1,0,4,3,2:T(8,128)(2,1)S(1)}, bf16[64,64,1,8,32]{1,0,4,3,2:T(8,128)(2,1)S(1)}) fusion(bf16[64,64,3,8,32]{1,0,4,3,2:T(8,128)(2,1)} %reshape.153), kind=kLoop, calls=%fused_computation.100 | loop fusion | bytes 12582912 | tf_op jit(solution)/shard_map/slice | solution.py:54
  143.7 21.2 %fusion.35 = f32[64,8,64,64]{2,3,1,0:T(8,128)} fusion(bf16[64,64,1,8,32]{1,0,4,3,2:T(8,128)(2,1)S(1)} %get-tuple-element.10, bf16[64,64,1,8,32]{1,0,4,3,2:T(8,128)(2,1)S(1)} %get-tuple-element.9), kind=kOutput, calls=%fused_computation.55 | convolution fusion | flops 134217728 | bytes 12582912 | tf_op jit(solution)/shard_map/gqhe,gkhe->ghqk/dot_general | solution.py:46
  164.9 17.7 %fusion.67 = (f32[64,8,64]{2,1,0:T(8,128)S(1)}, f32[64,8,64,64]{2,3,1,0:T(8,128)}) fusion(f32[64,8,64,64]{2,3,1,0:T(8,128)} %fusion.35, f32[8,64,64]{1,2,0:T(8,128)S(1)} %copy.132), kind=kOutput, calls=%fused_computation.103 | output fusion | flops 12582975 | bytes 17039360 | tf_op jit(solution)/shard_map/sub | solution.py:50
  182.7 18.1 %fusion.45 = bf16[64,8,32,64]{3,2,1,0:T(8,128)(2,1)} fusion(f32[64,8,64,64]{2,3,1,0:T(8,128)} %get-tuple-element.27, f32[64,8,64]{2,1,0:T(8,128)S(1)} %get-tuple-element.26, bf16[64,64,1,8,32]{1,0,4,3,2:T(8,128)(2,1)} %get-tuple-element.8), kind=kOutput, calls=%fused_computation.75 | convolution fusion | flops 139460608 | bytes 12713984 | tf_op jit(solution)/shard_map/ghqk,gkhe->gqhe/dot_general | solution.py:53
  200.7 4.8 %add_convert_fusion.1 = bf16[64,64,256]{2,1,0:T(8,128)(2,1)S(1)} fusion(f32[64,64,256]{2,1,0:T(8,128)} %bitcast.126, bf16[64,64,256]{1,2,0:T(8,128)(2,1)} %bitcast.138, bf16[256,256]{1,0:T(8,128)(2,1)S(1)} %copy-done.10), kind=kOutput, calls=%fused_computation.73 | convolution fusion | flops 538968064 | bytes 8519680 | tf_op jit(solution)/shard_map/dot_general | solution.py:56
  207.8 8.7 %all-to-all-start = ((bf16[2,128,8,2,256]{4,2,3,0,1:T(8,128)(2,1)}), bf16[2,128,8,2,256]{4,2,3,0,1:T(8,128)(2,1)S(1)}, u32[]{:S(2)}, u32[]{:S(2)}) async-start(bf16[2,128,8,2,256]{4,2,3,0,1:T(8,128)(2,1)} %copy.136), calls=%async_computation | async-start | bytes 4194304 | tf_op jit(solution)/shard_map/all_to_all | solution.py:113
  216.7 30.3 %all-to-all-done = bf16[2,128,8,2,256]{4,2,3,0,1:T(8,128)(2,1)S(1)} async-done(((bf16[2,128,8,2,256]{4,2,3,0,1:T(8,128)(2,1)}), bf16[2,128,8,2,256]{4,2,3,0,1:T(8,128)(2,1)S(1)}, u32[]{:S(2)}, u32[]{:S(2)}) %all-to-all-start) | async-done | bytes 2097184 | tf_op jit(solution)/shard_map/all_to_all | solution.py:113
  250.1 4.5 %copy.139 = f32[8,4,2,8,8,256]{5,4,3,2,1,0:T(8,128)} copy(f32[8,4,2,8,8,256]{5,0,2,1,4,3:T(8,128)S(1)} %bitcast.122) | data formatting | bytes 8388608 | tf_op jit(solution)/shard_map/convert_element_type | solution.py:120
  258.3 3.0 multiply_reduce_fusion
  261.9 4.6 %fusion.41 = bf16[4096,256]{1,0:T(8,128)(2,1)S(1)} fusion(f32[8,4,2,8,8,256]{5,4,3,2,1,0:T(8,128)} %copy.139, f32[256]{0:T(256)S(1)} %copy-done.14, f32[4096]{0:T(1024)S(1)} %sqrt.34, f32[4096]{0:T(1024)S(1)} %div.76), kind=kLoop, calls=%fused_computation.66 | loop fusion | flops 4194304 | bytes 6325248 | tf_op jit(solution)/shard_map/convert_element_type | solution.py:41
  266.5 4.5 %convolution_convert_fusion = bf16[4096,768]{1,0:T(8,128)(2,1)} fusion(bf16[4096,256]{1,0:T(8,128)(2,1)S(1)} %fusion.41, bf16[256,768]{1,0:T(8,128)(2,1)S(1)} %copy-done.7), kind=kOutput, calls=%fused_computation.39 | convolution fusion | flops 1613758464 | bytes 8781824 | tf_op jit(solution)/shard_map/dot_general | solution.py:42
  270.9 8.6 %copy.144 = bf16[4096,768]{0,1:T(8,128)(2,1)} copy(bf16[4096,768]{1,0:T(8,128)(2,1)} %convolution_convert_fusion) | data formatting | bytes 12582912 | tf_op jit(solution)/shard_map/convert_element_type | solution.py:42
  279.5 17.9 %reshape.157 = bf16[64,64,3,8,32]{1,0,4,3,2:T(8,128)(2,1)} reshape(bf16[4096,768]{0,1:T(8,128)(2,1)} %copy.144) | data formatting | bytes 12582912 | tf_op jit(solution)/shard_map/reshape | solution.py:45
  297.5 7.5 %fusion.63 = (bf16[64,64,1,8,32]{1,0,4,3,2:T(8,128)(2,1)}, bf16[64,64,1,8,32]{1,0,4,3,2:T(8,128)(2,1)S(1)}, bf16[64,64,1,8,32]{1,0,4,3,2:T(8,128)(2,1)S(1)}) fusion(bf16[64,64,3,8,32]{1,0,4,3,2:T(8,128)(2,1)} %reshape.157), kind=kLoop, calls=%fused_computation.99 | loop fusion | bytes 12582912 | tf_op jit(solution)/shard_map/slice | solution.py:54
  305.0 21.4 %fusion.34 = f32[64,8,64,64]{2,3,1,0:T(8,128)} fusion(bf16[64,64,1,8,32]{1,0,4,3,2:T(8,128)(2,1)S(1)} %get-tuple-element.7, bf16[64,64,1,8,32]{1,0,4,3,2:T(8,128)(2,1)S(1)} %get-tuple-element.6), kind=kOutput, calls=%fused_computation.51 | convolution fusion | flops 134217728 | bytes 12582912 | tf_op jit(solution)/shard_map/gqhe,gkhe->ghqk/dot_general | solution.py:46
  326.4 17.8 %fusion.68 = (f32[64,8,64]{2,1,0:T(8,128)S(1)}, f32[64,8,64,64]{2,3,1,0:T(8,128)}) fusion(f32[64,8,64,64]{2,3,1,0:T(8,128)} %fusion.34, f32[8,64,64]{1,2,0:T(8,128)S(1)} %copy.148), kind=kOutput, calls=%fused_computation.104 | output fusion | flops 12582975 | bytes 17039360 | tf_op jit(solution)/shard_map/sub | solution.py:50
  344.2 18.1 %fusion.44 = bf16[64,8,32,64]{3,2,1,0:T(8,128)(2,1)} fusion(f32[64,8,64,64]{2,3,1,0:T(8,128)} %get-tuple-element.29, f32[64,8,64]{2,1,0:T(8,128)S(1)} %get-tuple-element.28, bf16[64,64,1,8,32]{1,0,4,3,2:T(8,128)(2,1)} %get-tuple-element.5), kind=kOutput, calls=%fused_computation.74 | convolution fusion | flops 139460608 | bytes 12713984 | tf_op jit(solution)/shard_map/ghqk,gkhe->gqhe/dot_general | solution.py:53
  362.2 4.8 %add_convert_fusion = bf16[64,64,256]{2,1,0:T(8,128)(2,1)S(1)} fusion(f32[64,64,256]{2,1,0:T(8,128)} %bitcast.125, bf16[64,64,256]{1,2,0:T(8,128)(2,1)} %bitcast.139, bf16[256,256]{1,0:T(8,128)(2,1)S(1)} %copy-done.11), kind=kOutput, calls=%fused_computation.71 | convolution fusion | flops 538968064 | bytes 8519680 | tf_op jit(solution)/shard_map/dot_general | solution.py:56
  368.6 34.6 %all_to_all.10 = bf16[2,128,8,2,256]{4,2,3,0,1:T(8,128)(2,1)S(1)} all-to-all(bf16[2,128,8,2,256]{4,2,3,0,1:T(8,128)(2,1)S(1)} %copy.153), channel_id=1, replica_groups=mesh['lat'=4,'lon'=32] {'lat','lon'}, dimensions={1} | all-to-all | bytes 4194304 | tf_op jit(solution)/shard_map/all_to_all | solution.py:128
  (68 shorter events, 27.4 us)
Async XLA Ops:
  0.0 4.8 %copy-start = (bf16[256,1024]{1,0:T(8,128)(2,1)S(1)}, bf16[256,1024]{1,0:T(8,128)(2,1)}, u32[]{:S(2)}) copy-start(bf16[256,1024]{1,0:T(8,128)(2,1)} %param.15) | copy-start | bytes 1572868
  4.9 19.2 %copy-start.8 = (f32[8,64,64]{2,1,0:T(8,128)S(1)}, f32[8,64,64]{2,1,0:T(8,128)}, u32[]{:S(2)}) copy-start(f32[8,64,64]{2,1,0:T(8,128)} %param.20) | copy-start | bytes 393220
  12.7 3.2 copy-start.3
  15.9 26.3 %copy-start.12 = (f32[3,3,1024]{2,1,0:T(4,128)S(1)}, f32[3,3,1024]{2,1,0:T(4,128)}, u32[]{:S(2)}) copy-start(f32[3,3,1024]{2,1,0:T(4,128)} %param.16) | copy-start | bytes 110596
  15.9 8.3 %collective-permute-start = (bf16[1,64,1024]{2,1,0:T(8,128)(2,1)S(1)}, bf16[1,64,1024]{2,1,0:T(8,128)(2,1)S(1)}, u32[]{:S(2)}, u32[]{:S(2)}) collective-permute-start(bf16[1,64,1024]{2,1,0:T(8,128)(2,1)S(1)} %get-tuple-element.15), channel_id=1, source_target_pairs={{0,32},{32,64},{64,96},{1,33},{33,65},{65,97},{2,34},{34,66},{66,9... | collective-permute-start | bytes 393224 | tf_op jit(solution)/shard_map/ppermute | solution.py:14
  22.1 8.2 %collective-permute-start.1 = (bf16[1,64,1024]{2,1,0:T(8,128)(2,1)S(1)}, bf16[1,64,1024]{2,1,0:T(8,128)(2,1)S(1)}, u32[]{:S(2)}, u32[]{:S(2)}) collective-permute-start(bf16[1,64,1024]{2,1,0:T(8,128)(2,1)S(1)} %get-tuple-element.16), channel_id=1, source_target_pairs={{32,0},{64,32},{96,64},{33,1},{65,33},{97,65},{34,2},{66,34},{98,6... | collective-permute-start | bytes 393224 | tf_op jit(solution)/shard_map/ppermute | solution.py:17
  24.2 21.7 %copy-start.4 = (bf16[64,64,1024]{2,1,0:T(8,128)(2,1)S(1)}, bf16[64,64,1024]{2,1,0:T(8,128)(2,1)}, u32[]{:S(2)}) copy-start(bf16[64,64,1024]{2,1,0:T(8,128)(2,1)} %copy-done.3) | copy-start | bytes 25165828
  32.3 13.5 %collective-permute-start.2 = (bf16[66,1,1024]{2,1,0:T(2,128)(2,1)S(1)}, bf16[66,1,1024]{2,1,0:T(2,128)(2,1)S(1)}, u32[]{:S(2)}, u32[]{:S(2)}) collective-permute-start(bf16[66,1,1024]{2,1,0:T(2,128)(2,1)S(1)} %get-tuple-element.13), channel_id=1, source_target_pairs={{0,1},{1,2},{2,3},{3,4},{4,5},{5,6},{6,7},{7,8},{8,9},{9,10},{10,1... | collective-permute-start | bytes 405512 | tf_op jit(solution)/shard_map/ppermute | solution.py:14
  32.4 13.5 %collective-permute-start.3 = (bf16[66,1,1024]{2,1,0:T(2,128)(2,1)S(1)}, bf16[66,1,1024]{2,1,0:T(2,128)(2,1)S(1)}, u32[]{:S(2)}, u32[]{:S(2)}) collective-permute-start(bf16[66,1,1024]{2,1,0:T(2,128)(2,1)S(1)} %get-tuple-element.14), channel_id=1, source_target_pairs={{1,0},{2,1},{3,2},{4,3},{5,4},{6,5},{7,6},{8,7},{9,8},{10,9},{11,1... | collective-permute-start | bytes 405512 | tf_op jit(solution)/shard_map/ppermute | solution.py:17
  42.2 17.5 %copy-start.15 = (bf16[1024,256]{1,0:T(8,128)(2,1)S(1)}, bf16[1024,256]{1,0:T(8,128)(2,1)}, u32[]{:S(2)}) copy-start(bf16[1024,256]{1,0:T(8,128)(2,1)} %param.17) | copy-start | bytes 1572868
  91.8 6.7 %copy-start.5 = (bf16[64,64,256]{2,1,0:T(8,128)(2,1)S(1)}, bf16[64,64,256]{2,1,0:T(8,128)(2,1)}, u32[]{:S(2)}) copy-start(bf16[64,64,256]{2,1,0:T(8,128)(2,1)} %fusion.33) | copy-start | bytes 6291460
  91.8 8.4 %copy-start.13 = (f32[256]{0:T(256)S(1)}, f32[256]{0:T(256)}, u32[]{:S(2)}) copy-start(f32[256]{0:T(256)} %param.18) | copy-start | bytes 3076
  94.2 10.6 %copy-start.6 = (bf16[256,768]{1,0:T(8,128)(2,1)S(1)}, bf16[256,768]{1,0:T(8,128)(2,1)}, u32[]{:S(2)}) copy-start(bf16[256,768]{1,0:T(8,128)(2,1)} %param.19) | copy-start | bytes 1179652
  182.7 18.1 %copy-start.10 = (bf16[256,256]{1,0:T(8,128)(2,1)S(1)}, bf16[256,256]{1,0:T(8,128)(2,1)}, u32[]{:S(2)}) copy-start(bf16[256,256]{1,0:T(8,128)(2,1)} %param.21) | copy-start | bytes 393220
  205.5 11.0 %copy-start.9 = (f32[8,64,64]{2,1,0:T(8,128)S(1)}, f32[8,64,64]{2,1,0:T(8,128)}, u32[]{:S(2)}) copy-start(f32[8,64,64]{2,1,0:T(8,128)} %param.24) | copy-start | bytes 393220
  207.8 39.1 %all-to-all-start = ((bf16[2,128,8,2,256]{4,2,3,0,1:T(8,128)(2,1)}), bf16[2,128,8,2,256]{4,2,3,0,1:T(8,128)(2,1)S(1)}, u32[]{:S(2)}, u32[]{:S(2)}) async-start(bf16[2,128,8,2,256]{4,2,3,0,1:T(8,128)(2,1)} %copy.136), calls=%async_computation | async-start | bytes 4194304 | tf_op jit(solution)/shard_map/all_to_all | solution.py:113
  248.2 1.9 copy-start.2
  250.1 11.8 %copy-start.14 = (f32[256]{0:T(256)S(1)}, f32[256]{0:T(256)}, u32[]{:S(2)}) copy-start(f32[256]{0:T(256)} %param.22) | copy-start | bytes 3076
  254.6 11.9 %copy-start.7 = (bf16[256,768]{1,0:T(8,128)(2,1)S(1)}, bf16[256,768]{1,0:T(8,128)(2,1)}, u32[]{:S(2)}) copy-start(bf16[256,768]{1,0:T(8,128)(2,1)} %param.23) | copy-start | bytes 1179652
  344.1 18.1 %copy-start.11 = (bf16[256,256]{1,0:T(8,128)(2,1)S(1)}, bf16[256,256]{1,0:T(8,128)(2,1)}, u32[]{:S(2)}) copy-start(bf16[256,256]{1,0:T(8,128)(2,1)} %param.25) | copy-start | bytes 393220
  368.3 37.7 %copy-start.1 = (bf16[256,1024]{1,0:T(8,128)(2,1)S(1)}, bf16[256,1024]{1,0:T(8,128)(2,1)}, u32[]{:S(2)}) copy-start(bf16[256,1024]{1,0:T(8,128)(2,1)} %param.15) | copy-start | bytes 1572868
where the time goes:
time: 412 us; the launch traced here: 406 us
  matrix products  137 us (33%)
  local copies, waits for them, and re-layouts  91.5 us (22%)
  other arithmetic  75.8 us (18%)
  waiting for transfers between devices  40.1 us (10%)
  blocking collectives  34.6 us (8%)
  starting transfers between devices  26.6 us (6%)
    dot_general x2, matrix products, attend(): jnp.einsum('gqhe,gkhe->ghqk', qkv[:, :, 0], qkv[:, :, 1], preferred_eleme...  42.5 us
    dot_general x2, matrix products, attend(): jnp.einsum('ghqk,gkhe->gqhe', weights, qkv[:, :, 2], preferred_element_ty...  36.1 us
    reshape x2, local copies, waits for them, and re-layouts, attend(): qkv = qkv.reshape(groups, 64, 3, heads, head_size)  35.9 us
    sub x2, other arithmetic, attend(): scores = scores - jnp.max(scores, axis=-1, keepdims=True)  35.5 us
    all_to_all x1, blocking collectives, shards(): lax.all_to_all(outgoing, ('lat', 'lon'), split_axis=1, concat_axis=1, til...  34.6 us
    dot_general x1, matrix products, shards(): jnp.dot(conv, w_project, preferred_element_type=jnp.float32)  32.1 us
    all_to_all x1, waiting for transfers between devices, shards(): lax.all_to_all(flat, ('lat', 'lon'), split_axis=1, concat_axis=1, tiled=T...  30.3 us
    convert_element_type x2, local copies, waits for them, and re-layouts, attend(): jnp.dot(normed.reshape(-1, width), w_qkv, preferred_element_type=jnp.floa...  17.2 us
  transfers between devices with their start and end apart: 5, of which 3 were waited for; matrix products, arithmetic and copies ran while one was open for 0% of the time, Pallas kernels for 0%

commit v1 on v0

v1 whole, which is shorter than its diff:
```python
import functools

import jax
import jax.numpy as jnp
import numpy as np
from jax import lax
from jax.experimental import pallas as pl
from jax.experimental.pallas import tpu as pltpu
from jax.sharding import PartitionSpec as P

MESH = pl.DeviceIdType.MESH
BF16 = jnp.bfloat16
F32 = jnp.float32
ROWS, COLS, D, HID, HEADS = 64, 64, 256, 1024, 8
PHASES = 4
LOG2E = 1.4426950408889634


def dot(a, b):
    return jnp.dot(a, b, preferred_element_type=F32)


def dot_nt(a, b):
    return lax.dot_general(a, b, (((1,), (1,)), ((), ())), preferred_element_type=F32)


def gelu(x):
    half = x * BF16(0.5)
    inner = x * (BF16(0.7978845608) + BF16(0.035677408) * (x * x))
    return half + half * jnp.tanh(inner)


def norm(x, gain, average):
    xf = x.astype(F32)
    d = xf - dot(x, average)
    var = dot((d * d).astype(BF16), average)
    return (d * lax.rsqrt(var + 1e-05) * gain).astype(BF16)


def expand(x, gain, average, w_expand, store):
    n = norm(x, gain, average)
    for c in range(0, HID, 256):
        store(c, gelu(dot(n, w_expand[:, c : c + 256]).astype(BF16)))


def attend(x_ref, gain, average, w_qkv, bias, w_out, masks, select, ones_bd, qkv, mixed):
    n = norm(x_ref[...], gain[...], average[...])
    scale = LOG2E / 32**0.5
    qkv[:, 0:256] = (dot(n, w_qkv[:, 0:256]) * scale).astype(BF16)
    qkv[:, 256:512] = dot(n, w_qkv[:, 256:512]).astype(BF16)
    qkv[:, 512:768] = dot(n, w_qkv[:, 512:768]).astype(BF16)

    def blocks(m):
        return jnp.concatenate(
            [m[16 * i : 16 * i + 16] * masks[h] for i in range(4) for h in range(HEADS)], axis=0
        )

    def group(g, carry):
        rows = pl.ds(pl.multiple_of(g * 64, 64), 64)
        s = dot_nt(qkv[rows, 0:256], blocks(qkv[rows, 256:512])) + bias[...]
        top = jnp.maximum(
            jnp.maximum(s[:, 0:128], s[:, 128:256]), jnp.maximum(s[:, 256:384], s[:, 384:512])
        )
        for shift in (8, 4, 2, 1):
            top = jnp.maximum(top, pltpu.roll(top, 128 - shift, 1))
        high = top.astype(BF16)
        low = (top - high.astype(F32)).astype(BF16)
        top = dot(jnp.concatenate([high, low], axis=1), select[...])
        p = jnp.concatenate(
            [jnp.exp2(s[:, 128 * i : 128 * i + 128] - top).astype(BF16) for i in range(4)], axis=1
        )
        value = dot(p, blocks(qkv[rows, 512:768]))
        total = dot(p, ones_bd[...])
        mixed[rows, :] = (value / total).astype(BF16)
        return carry

    lax.fori_loop(0, 8, group, 0, unroll=4)
    return dot(mixed[...], w_out[...])


def kernel(
    tokens,
    edge_left,
    edge_right,
    gain_conv,
    w_expand,
    dw16,
    dw_edge,
    w_project,
    gain_block,
    qkv_block,
    bias_block,
    out_block,
    gain_grid,
    qkv_grid,
    bias_grid,
    out_grid,
    average,
    masks,
    select,
    ones_bd,
    shifts,
    edge_shift,
    perm,
    out,
    e_mid,
    e_edge,
    halo_row,
    halo_col,
    edge_sum,
    conv,
    mixed,
    qkv,
    att,
    blocked,
    received,
    outgoing,
    halo_send,
    halo_recv,
    send_sem,
    recv_sem,
    back_send,
    back_recv,
):
    lat = lax.axis_index("lat")
    lon = lax.axis_index("lon")
    lats = lax.axis_size("lat")
    lons = lax.axis_size("lon")
    kind = lax.rem(lon, 4)
    place = lon // 4
    far = 3 - kind
    mine = lat * 8 + place
    my_row, my_col = mine // 4, lax.rem(mine, 4)
    west = lax.rem(lon + lons - 1, lons)
    east = lax.rem(lon + 1, lons)

    def partner(i):
        return {"lat": i // 8, "lon": lax.rem(i, 8) * 4 + far}

    barrier = pltpu.get_barrier_semaphore()

    def greet(i, carry):
        pl.semaphore_signal(barrier, inc=1, device_id=partner(i), device_id_type=MESH)
        return carry

    lax.fori_loop(0, 32, greet, 0)
    for side in (west, east):
        pl.semaphore_signal(
            barrier, inc=1, device_id={"lat": lat, "lon": side}, device_id_type=MESH
        )

    @pl.when(lat > 0)
    def _():
        for side in (lon, west, east):
            pl.semaphore_signal(
                barrier, inc=1, device_id={"lat": lat - 1, "lon": side}, device_id_type=MESH
            )

    @pl.when(lat < lats - 1)
    def _():
        for side in (lon, west, east):
            pl.semaphore_signal(
                barrier, inc=1, device_id={"lat": lat + 1, "lon": side}, device_id_type=MESH
            )

    inner = jnp.minimum(lat, 1) + jnp.minimum(lats - 1 - lat, 1)
    pl.semaphore_wait(barrier, 34 + 3 * inner)

    def halo(slot, src, dst, to_lat, to_lon):
        return pltpu.make_async_remote_copy(
            src_ref=src,
            dst_ref=dst,
            send_sem=halo_send.at[slot],
            recv_sem=halo_recv.at[slot],
            device_id={"lat": to_lat, "lon": to_lon},
            device_id_type=MESH,
        )

    to_west = halo(0, edge_left, halo_col.at[1, pl.ds(16, 64)], lat, west)
    to_east = halo(1, edge_right, halo_col.at[0, pl.ds(16, 64)], lat, east)
    north = [
        halo(2, tokens.at[0], halo_row.at[1], lat - 1, lon),
        halo(3, edge_left.at[pl.ds(0, 16)], halo_col.at[1, pl.ds(80, 16)], lat - 1, west),
        halo(4, edge_right.at[pl.ds(0, 16)], halo_col.at[0, pl.ds(80, 16)], lat - 1, east),
    ]
    south = [
        halo(5, tokens.at[ROWS - 1], halo_row.at[0], lat + 1, lon),
        halo(6, edge_left.at[pl.ds(48, 16)], halo_col.at[1, pl.ds(0, 16)], lat + 1, west),
        halo(7, edge_right.at[pl.ds(48, 16)], halo_col.at[0, pl.ds(0, 16)], lat + 1, east),
    ]
    to_west.start()
    to_east.start()

    @pl.when(lat > 0)
    def _():
        for c in north:
            c.start()

    @pl.when(lat < lats - 1)
    def _():
        for c in south:
            c.start()

    @pl.when(lat == 0)
    def _():
        halo_row[0] = jnp.zeros((COLS, D), BF16)
        halo_col[0, 0:16] = jnp.zeros((16, D), BF16)
        halo_col[1, 0:16] = jnp.zeros((16, D), BF16)

    @pl.when(lat == lats - 1)
    def _():
        halo_row[1] = jnp.zeros((COLS, D), BF16)
        halo_col[0, 80:96] = jnp.zeros((16, D), BF16)
        halo_col[1, 80:96] = jnp.zeros((16, D), BF16)

    def expand_rows(first, count):
        def store(c, v):
            e_mid[pl.ds(first + 1, count), :, c : c + 256] = v.reshape(count, COLS, 256)

        x = tokens[pl.ds(first, count)].reshape(count * COLS, D)
        expand(x, gain_conv[...], average[...], w_expand, store)

    expand_rows(0, 1)
    expand_rows(31, 2)

    to_west.wait()
    to_east.wait()

    @pl.when(lat > 0)
    def _():
        for c in north:
            c.wait_send()
        for c in south:
            c.wait_recv()

    @pl.when(lat < lats - 1)
    def _():
        for c in south:
            c.wait_send()
        for c in north:
            c.wait_recv()

    def store_rows(c, v):
        e_mid[0, :, c : c + 256] = v[0:64]
        e_mid[65, :, c : c + 256] = v[64:128]

    expand(halo_row[...].reshape(2 * COLS, D), gain_conv[...], average[...], w_expand, store_rows)

    def store_cols(c, v):
        e_edge[:, c : c + 256] = v

    expand(halo_col[...].reshape(192, D), gain_conv[...], average[...], w_expand, store_cols)
    for c in range(0, HID, 256):
        total = jnp.zeros((8, 16, 256), F32)
        for dy in range(3):
            moved = dot(edge_shift[dy], e_edge[:, c : c + 256]).reshape(8, 16, 256)
            total = total + moved * dw_edge[dy, :, c : c + 256][None]
        edge_sum[:, :, c : c + 256] = total.astype(BF16)

    def conv_band(band):
        first = band * 8

        def row(r, carry):
            for c in range(0, HID, 256):
                parts = []
                e = [e_mid[first + r + dy, :, c : c + 256] for dy in range(3)]
                for dx in range(3):
                    acc = None
                    for dy in range(3):
                        w = dw16[3 * dy + dx, :, c : c + 256]
                        w = jnp.concatenate([w] * 4, axis=0)
                        term = e[dy] * w
                        acc = term if acc is None else acc + term
                    parts.append(acc)
                parts.append(edge_sum[band, :, c : c + 256])
                total = dot(shifts[r], jnp.concatenate(parts, axis=0))
                conv[pl.ds(r * 64, 64), c : c + 256] = gelu(total.astype(BF16))
            return carry

        lax.fori_loop(0, 8, row, 0, unroll=2)

    def pieces(x):
        return jnp.concatenate(
            [x[64 * b + 8 * a : 64 * b + 8 * a + 8] for a in range(8) for b in range(8)], axis=0
        )

    def send(phase):
        def one(i, carry):
            pltpu.make_async_remote_copy(
                src_ref=blocked.at[
                    :, phase * 8 + i // 4, pl.ds(pl.multiple_of(lax.rem(i, 4) * 16, 16), 16), :
                ],
                dst_ref=received.at[phase, lat, :, place],
                send_sem=send_sem.at[phase],
                recv_sem=recv_sem.at[phase],
                device_id=partner(i),
                device_id_type=MESH,
            ).start()
            return carry

        lax.fori_loop(0, 32, one, 0)

    def send_back(phase):
        def one(i, carry):
            pltpu.make_async_remote_copy(
                src_ref=outgoing.at[phase, i // 8, :, lax.rem(i, 8)],
                dst_ref=out.at[
                    :, phase * 8 + my_row, pl.ds(pl.multiple_of(my_col * 16, 16), 16), :
                ],
                send_sem=back_send.at[phase],
                recv_sem=back_recv.at[phase],
                device_id=partner(i),
                device_id_type=MESH,
            ).start()
            return carry

        lax.fori_loop(0, 32, one, 0)

    def conv_and_block(phase):
        def half(i, carry):
            band = i * 4 + phase
            first = band * 8

            @pl.when(band < 7)
            def _():
                expand_rows(first + 1, 8)

            @pl.when(band == 7)
            def _():
                expand_rows(first + 1, 7)

            conv_band(band)
            x = tokens[pl.ds(first, 8)].reshape(512, D).astype(F32)
            mixed[...] = pieces(x + dot(conv[0:512], w_project[...])).astype(BF16)
            result = attend(
                mixed, gain_block, average, qkv_block, bias_block, out_block, masks, select,
                ones_bd, qkv, att,
            )
            blocked[i, pl.ds(phase * 8, 8)] = (
                pieces(result + mixed[...].astype(F32)).astype(BF16).reshape(8, 64, D)
            )
            return carry

        lax.fori_loop(0, 2, half, 0)

    def grid(phase):
        for half in range(2):
            for q in range(4):
                x = received[phase, q].reshape(256, D)
                y = dot(perm[128 * half : 128 * half + 128], x).astype(BF16)
                for p in range(8):
                    mixed[64 * p + 16 * q : 64 * p + 16 * q + 16] = y[16 * p : 16 * p + 16]
            result = attend(
                mixed, gain_grid, average, qkv_grid, bias_grid, out_grid, masks, select, ones_bd,
                qkv, att,
            )
            done = (result + mixed[...].astype(F32)).astype(BF16)
            for q in range(4):
                conv[256 * q + 128 * half : 256 * q + 128 * half + 128, 0:256] = jnp.concatenate(
                    [done[64 * p + 16 * q : 64 * p + 16 * q + 16] for p in range(8)], axis=0
                )
        for q in range(4):
            y = dot(perm[...], conv[256 * q : 256 * q + 256, 0:256]).astype(BF16)
            outgoing[phase, q] = y.reshape(2, 8, 16, D)

    def wait_all(ref, sem):
        pltpu.make_async_copy(ref, ref, sem).wait()

    def step(phase, carry):
        @pl.when(phase < PHASES)
        def _():
            conv_and_block(phase)
            send(phase)

        @pl.when(phase > 0)
        def _():
            wait_all(received.at[phase - 1], recv_sem.at[phase - 1])
            grid(phase - 1)
            send_back(phase - 1)

        return carry

    lax.fori_loop(0, PHASES + 1, step, 0)

    def finish(phase, carry):
        wait_all(received.at[phase], send_sem.at[phase])
        wait_all(received.at[phase], back_send.at[phase])
        wait_all(received.at[phase], back_recv.at[phase])
        return carry

    lax.fori_loop(0, PHASES, finish, 0)


def constants():
    average = np.full((D, D), 1.0 / D, np.float32)
    lane_head = np.arange(D) // 32
    masks = np.zeros((HEADS, 16, D), np.float32)
    for h in range(HEADS):
        masks[h, :, lane_head == h] = 1.0
    select = np.zeros((256, 128), np.float32)
    for c in range(128):
        select[c // 16 * 16, c] = 1.0
        select[128 + c // 16 * 16, c] = 1.0
    ones_bd = np.zeros((512, D), np.float32)
    row_head = np.arange(512) // 16 % 8
    ones_bd[row_head[:, None] == lane_head[None, :]] = 1.0
    shifts = np.zeros((8, 64, 208), np.float32)
    for r in range(8):
        for c in range(64):
            if c > 0:
                shifts[r, c, c - 1] = 1.0
            shifts[r, c, 64 + c] = 1.0
            if c < 63:
                shifts[r, c, 128 + c + 1] = 1.0
        shifts[r, 0, 192 + r] = 1.0
        shifts[r, 63, 200 + r] = 1.0
    edge_shift = np.zeros((3, 128, 192), np.float32)
    for dy in range(3):
        for band in range(8):
            for side in range(2):
                for r in range(8):
                    edge_shift[dy, band * 16 + side * 8 + r, side * 96 + 16 + band * 8 + r + dy - 1] = 1
    perm = np.zeros((256, 256), np.float32)
    for p in range(16):
        for s in range(16):
            perm[p * 16 + s, s * 16 + p] = 1.0
    return [
        jnp.asarray(a, BF16)
        for a in (average, masks, select, ones_bd, shifts, edge_shift, perm)
    ]


def spread_bias(bias):
    return (
        (bias * LOG2E).reshape(HEADS, 64, 4, 16).transpose(1, 2, 0, 3).reshape(64, 512)
    )


def shards(
    tokens,
    gain_conv,
    w_expand,
    dw_kernel,
    w_project,
    gain_block,
    qkv_block,
    bias_block,
    out_block,
    gain_grid,
    qkv_grid,
    bias_grid,
    out_grid,
):
    dw16 = jnp.broadcast_to(dw_kernel.astype(BF16).reshape(9, 1, HID), (9, 16, HID))
    dw_edge = jnp.repeat(dw_kernel[:, 0::2, :], 8, axis=1)
    operands = [
        tokens,
        tokens[:, 0],
        tokens[:, COLS - 1],
        gain_conv.reshape(1, D),
        w_expand,
        dw16,
        dw_edge,
        w_project,
        gain_block.reshape(1, D),
        qkv_block,
        spread_bias(bias_block),
        out_block,
        gain_grid.reshape(1, D),
        qkv_grid,
        spread_bias(bias_grid),
        out_grid,
        *constants(),
    ]
    result = pl.pallas_call(
        kernel,
        out_shape=jax.ShapeDtypeStruct((2, 32, COLS, D), BF16),
        in_specs=[pl.BlockSpec(memory_space=pltpu.VMEM)] * len(operands),
        out_specs=pl.BlockSpec(memory_space=pltpu.VMEM),
        scratch_shapes=[
            pltpu.VMEM((66, COLS, HID), BF16),
            pltpu.VMEM((192, HID), BF16),
            pltpu.VMEM((2, COLS, D), BF16),
            pltpu.VMEM((2, 96, D), BF16),
            pltpu.VMEM((8, 16, HID), BF16),
            pltpu.VMEM((1024, HID), BF16),
            pltpu.VMEM((512, D), BF16),
            pltpu.VMEM((512, 3 * D), BF16),
            pltpu.VMEM((512, D), BF16),
            pltpu.VMEM((2, 32, COLS, D), BF16),
            pltpu.VMEM((PHASES, 4, 2, 8, 16, D), BF16),
            pltpu.VMEM((PHASES, 4, 2, 8, 16, D), BF16),
            pltpu.SemaphoreType.DMA((8,)),
            pltpu.SemaphoreType.DMA((8,)),
            pltpu.SemaphoreType.DMA((PHASES,)),
            pltpu.SemaphoreType.DMA((PHASES,)),
            pltpu.SemaphoreType.DMA((PHASES,)),
            pltpu.SemaphoreType.DMA((PHASES,)),
        ],
        compiler_params=pltpu.CompilerParams(
            collective_id=0, has_side_effects=True, vmem_limit_bytes=60 * 1024 * 1024
        ),
    )(*operands)
    return result.reshape(ROWS, COLS, D)


def solution(mesh):
    placed = (P("lat", "lon", None), P(), P(), P(), P(), P(), P(), P(), P(), P(), P(), P(), P())
    return jax.shard_map(
        shards, mesh=mesh, in_specs=placed, out_specs=P("lat", "lon", None), check_vma=False
    )
```

time: 412 us -> 171 us (0.42); the launches traced: 406 us -> 171 us
  Pallas kernels: 0 us -> 160 us
  matrix products: 137 us -> 0 us
  local copies, waits for them, and re-layouts: 91.5 us -> 10.7 us
  other arithmetic: 75.8 us -> 0.86 us
  waiting for transfers between devices: 40.1 us -> 0 us
  blocking collectives: 34.6 us -> 0 us
  starting transfers between devices: 26.6 us -> 0 us
    pallas_call x0 -> x1, Pallas kernels: none -> 160 us  [shards(): pl.pallas_call(kernel, out_shape=jax.ShapeDtypeStruct((2, 32, COLS, D), B...]
    dot_general x10 -> x0, matrix products: 137 us -> none  [the longest x2 42.5 us: attend(): jnp.einsum('gqhe,gkhe->ghqk', qkv[:, :, 0], qkv[:, :, 1], preferred_eleme...]
    reshape x7 -> x3, local copies, waits for them, and re-layouts: 42.2 us -> 2.24 us  [the longest x2 1.54 us: spread_bias(): (bias * LOG2E).reshape(HEADS, 64, 4, 16).transpose(1, 2, 0, 3)]
    sub x2 -> x0, other arithmetic: 35.5 us -> none  [attend(): scores = scores - jnp.max(scores, axis=-1, keepdims=True)]
    all_to_all x1 -> x0, blocking collectives: 34.6 us -> none  [shards(): lax.all_to_all(outgoing, ('lat', 'lon'), split_axis=1, concat_axis=1, til...]
    all_to_all x1 -> x0, waiting for transfers between devices: 30.3 us -> none  [shards(): lax.all_to_all(flat, ('lat', 'lon'), split_axis=1, concat_axis=1, tiled=T...]
    convert_element_type x5 -> x0, local copies, waits for them, and re-layouts: 26.3 us -> none  [the longest x2 17.2 us: attend(): jnp.dot(normed.reshape(-1, width), w_qkv, preferred_element_type=jnp.floa...]
    ppermute x4 -> x0, starting transfers between devices: 18 us -> none  [the longest x2 11.7 us: padded_2(): lax.ppermute(lax.slice_in_dim(block, 0, width, axis=dim), axis, backward)]
  transfers between devices with their start and end apart: 5 -> 0, of which waited for: 3 -> 0; matrix products, arithmetic and copies ran while one was open for 0% -> 0% of each run, Pallas kernels for 0% -> 0%
where the time goes in v1:
time: 171 us
  Pallas kernels  160 us (94%)
  local copies, waits for them, and re-layouts  10.7 us (6%)
    pallas_call x1, Pallas kernels, shards(): pl.pallas_call(kernel, out_shape=jax.ShapeDtypeStruct((2, 32, COLS, D), B...  160 us
    unnamed x5, local copies, waits for them, and re-layouts  4.37 us

profile of v1, /device:TPU:1, one launch (start us, length us, event | category | flops | bytes accessed | tf_op | source)
XLA Modules:
  0.0 171.2 jit_solution(13007832510098933110)
XLA Ops:
  0.0 0.0 copy-start
  0.0 0.9 slice.11
  0.9 0.8 convert_element_type.3
  1.7 1.1 fusion
  2.9 0.6 copy_bitcast_fusion
  3.5 0.7 broadcast_bitcast_fusion.dw_edge
  4.2 0.7 broadcast_in_dim.11.dw16
  4.9 1.1 copy.27
  6.1 0.8 copy.31.bias_block
  6.9 0.0 copy-done
  6.9 0.1 copy.29
  7.1 0.8 copy.32.bias_grid
  7.8 0.7 jit_solution_.3.average
  8.5 159.6 %shard_map.190 = bf16[2,32,64,256]{3,2,1,0:T(8,128)(2,1)} custom-call(bf16[64,64,256]{2,1,0:T(8,128)(2,1)} %tokens.1, bf16[64,256]{1,0:T(8,128)(2,1)} %get-tuple-element.8.edge_left, bf16[64,256]{1,0:T(8,128)(2,1)} %get-tuple-element.7.edge_right, f32[1,256]{1,0:T(1,128)} %bitcast.23, bf16[256,1024]{1,0:T(8,128)(2,1)} %w_expand.1, ...), custom_call_target="tpu_custom_call" | custom-call | tf_op jit(solution)/shard_map/pallas_call | solution.py:475
  168.1 3.2 %copy.38 = bf16[64,64,256]{2,1,0:T(8,128)(2,1)} copy(bf16[64,64,256]{2,1,0:T(8,128)(2,1)} %bitcast.18) | data formatting | bytes 4194304
  (5 shorter events, 0.1 us)
Async XLA Ops:
  0.0 6.9 %copy-start = (f32[8,64,64]{2,1,0:T(8,128)S(1)}, f32[8,64,64]{2,1,0:T(8,128)}, u32[]{:S(2)}) copy-start(f32[8,64,64]{2,1,0:T(8,128)} %param.31) | copy-start | bytes 393220

commit v2 on v1

--- a/solution.py
+++ b/solution.py
@@ -13,6 +13,7 @@
 F32 = jnp.float32
 ROWS, COLS, D, HID, HEADS = 64, 64, 256, 1024, 8
 PHASES = 4
+BATCH = 8
 LOG2E = 1.4426950408889634
 
 
@@ -22,6 +23,10 @@
 
 def dot_nt(a, b):
     return lax.dot_general(a, b, (((1,), (1,)), ((), ())), preferred_element_type=F32)
+
+
+def exp2(x):
+    return jnp.exp2(x)
 
 
 def gelu(x):
@@ -41,6 +46,20 @@
     n = norm(x, gain, average)
     for c in range(0, HID, 256):
         store(c, gelu(dot(n, w_expand[:, c : c + 256]).astype(BF16)))
+
+
+def blocks(m, masks):
+    return jnp.concatenate(
+        [m[16 * i : 16 * i + 16] * masks[h] for i in range(4) for h in range(HEADS)], axis=0
+    )
+
+
+def head_top(top, select):
+    for shift in (8, 4, 2, 1):
+        top = jnp.maximum(top, pltpu.roll(top, 128 - shift, 1))
+    high = top.astype(BF16)
+    low = (top - high.astype(F32)).astype(BF16)
+    return dot(jnp.concatenate([high, low], axis=1), select[...])
 
 
 def attend(x_ref, gain, average, w_qkv, bias, w_out, masks, select, ones_bd, qkv, mixed):
@@ -50,31 +69,33 @@
     qkv[:, 256:512] = dot(n, w_qkv[:, 256:512]).astype(BF16)
     qkv[:, 512:768] = dot(n, w_qkv[:, 512:768]).astype(BF16)
 
-    def blocks(m):
-        return jnp.concatenate(
-            [m[16 * i : 16 * i + 16] * masks[h] for i in range(4) for h in range(HEADS)], axis=0
-        )
-
-    def group(g, carry):
-        rows = pl.ds(pl.multiple_of(g * 64, 64), 64)
-        s = dot_nt(qkv[rows, 0:256], blocks(qkv[rows, 256:512])) + bias[...]
-        top = jnp.maximum(
-            jnp.maximum(s[:, 0:128], s[:, 128:256]), jnp.maximum(s[:, 256:384], s[:, 384:512])
-        )
-        for shift in (8, 4, 2, 1):
-            top = jnp.maximum(top, pltpu.roll(top, 128 - shift, 1))
-        high = top.astype(BF16)
-        low = (top - high.astype(F32)).astype(BF16)
-        top = dot(jnp.concatenate([high, low], axis=1), select[...])
-        p = jnp.concatenate(
-            [jnp.exp2(s[:, 128 * i : 128 * i + 128] - top).astype(BF16) for i in range(4)], axis=1
-        )
-        value = dot(p, blocks(qkv[rows, 512:768]))
-        total = dot(p, ones_bd[...])
-        mixed[rows, :] = (value / total).astype(BF16)
+    def batch(b, carry):
+        rows = [pl.ds(pl.multiple_of((b * BATCH + i) * 64, 64), 64) for i in range(BATCH)]
+        scores = [dot_nt(qkv[r, 0:256], blocks(qkv[r, 256:512], masks)) + bias[...] for r in rows]
+        tops = [
+            jnp.maximum(
+                jnp.maximum(s[:, 0:128], s[:, 128:256]), jnp.maximum(s[:, 256:384], s[:, 384:512])
+            )
+            for s in scores
+        ]
+        top = head_top(jnp.concatenate(tops, axis=0), select)
+        weights = [
+            jnp.concatenate(
+                [
+                    exp2(s[:, 128 * i : 128 * i + 128] - top[64 * k : 64 * k + 64]).astype(BF16)
+                    for i in range(4)
+                ],
+                axis=1,
+            )
+            for k, s in enumerate(scores)
+        ]
+        values = [dot(p, blocks(qkv[r, 512:768], masks)) for p, r in zip(weights, rows)]
+        total = dot(jnp.concatenate(weights, axis=0), ones_bd[...])
+        whole = pl.ds(pl.multiple_of(b * (BATCH * 64), 64), BATCH * 64)
+        mixed[whole, :] = (jnp.concatenate(values, axis=0) / total).astype(BF16)
         return carry
 
-    lax.fori_loop(0, 8, group, 0, unroll=4)
+    lax.fori_loop(0, 8 // BATCH, batch, 0)
     return dot(mixed[...], w_out[...])
 
 

time: 171 us -> 110 us (0.64)
  Pallas kernels: 160 us -> 98.4 us
    pallas_call x1, Pallas kernels: 160 us -> 98.4 us  [shards(): pl.pallas_call(kernel, out_shape=jax.ShapeDtypeStruct((2, 32, COLS, D), B...]
where the time goes in v2:
time: 110 us
  Pallas kernels  98.4 us (89%)
  local copies, waits for them, and re-layouts  10.7 us (10%)
    pallas_call x1, Pallas kernels, shards(): pl.pallas_call(kernel, out_shape=jax.ShapeDtypeStruct((2, 32, COLS, D), B...  98.4 us
    unnamed x5, local copies, waits for them, and re-layouts  4.37 us

profile of v2, /device:TPU:1, one launch (start us, length us, event | category | flops | bytes accessed | tf_op | source)
XLA Modules:
  0.0 110.1 jit_solution(12974140133952063646)
XLA Ops:
  0.0 0.0 copy-start
  0.0 0.9 slice.11
  0.9 0.8 convert_element_type.3
  1.7 1.1 %fusion = (bf16[64,1,256]{2,1,0:T(2,128)(2,1)S(1)}, bf16[64,1,256]{2,1,0:T(2,128)(2,1)S(1)}) fusion(bf16[64,64,256]{2,1,0:T(8,128)(2,1)} %tokens.1), kind=kLoop, calls=%fused_computation.5 | loop fusion | bytes 131072 | tf_op jit(solution)/shard_map/slice | solution.py:480
  2.9 0.6 copy_bitcast_fusion
  3.5 0.7 broadcast_bitcast_fusion.dw_edge
  4.2 0.7 broadcast_in_dim.11.dw16
  4.9 1.1 copy.27
  6.1 0.8 copy.31.bias_block
  6.9 0.0 copy-done
  6.9 0.1 copy.29
  7.1 0.8 copy.32.bias_grid
  7.8 0.7 jit_solution_.3.average
  8.5 98.4 %shard_map.190 = bf16[2,32,64,256]{3,2,1,0:T(8,128)(2,1)} custom-call(bf16[64,64,256]{2,1,0:T(8,128)(2,1)} %tokens.1, bf16[64,256]{1,0:T(8,128)(2,1)} %get-tuple-element.8.edge_left, bf16[64,256]{1,0:T(8,128)(2,1)} %get-tuple-element.7.edge_right, f32[1,256]{1,0:T(1,128)} %bitcast.23, bf16[256,1024]{1,0:T(8,128)(2,1)} %w_expand.1, ...), custom_call_target="tpu_custom_call" | custom-call | tf_op jit(solution)/shard_map/pallas_call | solution.py:496
  106.9 3.2 %copy.38 = bf16[64,64,256]{2,1,0:T(8,128)(2,1)} copy(bf16[64,64,256]{2,1,0:T(8,128)(2,1)} %bitcast.18) | data formatting | bytes 4194304
  (5 shorter events, 0.1 us)
Async XLA Ops:
  0.0 6.9 %copy-start = (f32[8,64,64]{2,1,0:T(8,128)S(1)}, f32[8,64,64]{2,1,0:T(8,128)}, u32[]{:S(2)}) copy-start(f32[8,64,64]{2,1,0:T(8,128)} %param.31) | copy-start | bytes 393220

commit v3 on v2

v3 whole, which is shorter than its diff:
```python
import jax
import jax.numpy as jnp
from jax import lax
from jax.experimental import pallas as pl
from jax.experimental.pallas import tpu as pltpu
from jax.sharding import PartitionSpec as P

MESH = pl.DeviceIdType.MESH
BF16 = jnp.bfloat16
F32 = jnp.float32
ROWS, COLS, D, HID, HEADS = 64, 64, 256, 1024, 8
PHASES = 4
BATCH = 16
LOG2E = 1.4426950408889634


def dot(a, b):
    return jnp.dot(a, b, preferred_element_type=F32)


def dot_nt(a, b):
    return lax.dot_general(a, b, (((1,), (1,)), ((), ())), preferred_element_type=F32)


def exp2(x):
    return jnp.exp2(x)


def gelu(x):
    half = x * BF16(0.5)
    inner = x * (BF16(0.7978845608) + BF16(0.035677408) * (x * x))
    return half + half * jnp.tanh(inner)


def norm(x, gain):
    xf = x.astype(F32)
    d = xf - jnp.mean(xf, axis=-1, keepdims=True)
    var = jnp.mean(d * d, axis=-1, keepdims=True)
    return (d * lax.rsqrt(var + 1e-05) * gain).astype(BF16)


def expand(x, gain, w_expand, store):
    n = norm(x, gain)
    for c in range(0, HID, 256):
        store(c, gelu(dot(n, w_expand[:, c : c + 256]).astype(BF16)))


def blocks(m, masks):
    return jnp.concatenate(
        [m[16 * i : 16 * i + 16] * masks[h] for i in range(4) for h in range(4)], axis=0
    )


def head_top(pairs, select):
    wide = [jnp.maximum(x, pltpu.roll(x, 64, 1)) for x in pairs]
    lane = lax.broadcasted_iota(jnp.int32, wide[0].shape, 1)
    top = jnp.where(lane < 64, wide[0], wide[1])
    for shift in (8, 4, 2, 1):
        top = jnp.maximum(top, pltpu.roll(top, 128 - shift, 1))
    high = top.astype(BF16)
    low = (top - high.astype(F32)).astype(BF16)
    return dot(jnp.concatenate([high, low], axis=1), select[...])


def attend(x_ref, gain, w_qkv, bias, w_out, masks, select, ones_bd, qkv, mixed):
    n = norm(x_ref[...], gain[...])
    scale = LOG2E / 32**0.5
    qkv[:, 0:256] = (dot(n, w_qkv[:, 0:256]) * scale).astype(BF16)
    qkv[:, 256:512] = dot(n, w_qkv[:, 256:512]).astype(BF16)
    qkv[:, 512:768] = dot(n, w_qkv[:, 512:768]).astype(BF16)
    size = BATCH * 64

    def batch(first):
        rows = [pl.ds(first + i * 64, 64) for i in range(BATCH)]
        scores = [
            jnp.concatenate(
                [
                    dot_nt(
                        qkv[r, 128 * u : 128 * u + 128],
                        blocks(qkv[r, 256 + 128 * u : 384 + 128 * u], masks),
                    )
                    + bias[:, 256 * u : 256 * u + 256]
                    for r in rows
                ],
                axis=0,
            )
            for u in range(2)
        ]
        top = head_top([jnp.maximum(s[:, 0:128], s[:, 128:256]) for s in scores], select)
        weights, sums = [], []
        for u, s in enumerate(scores):
            t = top[:, 128 * u : 128 * u + 128]
            a, b = exp2(s[:, 0:128] - t), exp2(s[:, 128:256] - t)
            sums.append((a + b).astype(BF16))
            weights.append(jnp.concatenate([a.astype(BF16), b.astype(BF16)], axis=1))
        total = dot(jnp.concatenate(sums, axis=1), ones_bd[...])
        values = jnp.concatenate(
            [
                jnp.concatenate(
                    [
                        dot(
                            w[64 * k : 64 * k + 64],
                            blocks(qkv[r, 512 + 128 * u : 640 + 128 * u], masks),
                        )
                        for k, r in enumerate(rows)
                    ],
                    axis=0,
                )
                for u, w in enumerate(weights)
            ],
            axis=1,
        )
        mixed[pl.ds(first, size), :] = (values / total).astype(BF16)

    for first in range(0, x_ref.shape[0], size):
        batch(first)
    return dot(mixed[...], w_out[...])


def spread_bias(source, target):
    lane = lax.broadcasted_iota(jnp.int32, (64, 128), 1)
    for u in range(2):
        twice = []
        for h in range(4):
            x = source[4 * u + h] * LOG2E
            twice.append(jnp.concatenate([x, x], axis=1))
        for tile in range(2):
            acc = twice[0]
            for k in range(2):
                for h in range(4):
                    at, to = (2 * tile + k) * 16, k * 64 + h * 16
                    moved = pltpu.roll(twice[h], (to - at) % 128, 1)
                    acc = jnp.where(lane // 16 == to // 16, moved, acc)
            target[:, 256 * u + 128 * tile : 256 * u + 128 * tile + 128] = acc


def pick(shape, hit):
    row = lax.broadcasted_iota(jnp.int32, shape, 0)
    col = lax.broadcasted_iota(jnp.int32, shape, 1)
    return jnp.where(hit(row, col), 1.0, 0.0).astype(BF16)


def kernel(
    tokens,
    gain_conv,
    w_expand,
    dw_kernel,
    w_project,
    gain_block,
    qkv_block,
    bias_in_block,
    out_block,
    gain_grid,
    qkv_grid,
    bias_in_grid,
    out_grid,
    out,
    e_mid,
    e_edge,
    halo_row,
    halo_col,
    edge,
    edge_sum,
    dw16,
    bias_block,
    bias_grid,
    masks,
    select,
    ones_bd,
    shifts,
    edge_shift,
    perm,
    conv,
    mixed,
    qkv,
    att,
    blocked,
    received,
    outgoing,
    halo_send,
    halo_recv,
    send_sem,
    recv_sem,
    back_send,
    back_recv,
):
    lat = lax.axis_index("lat")
    lon = lax.axis_index("lon")
    lats = lax.axis_size("lat")
    lons = lax.axis_size("lon")
    kind = lax.rem(lon, 4)
    place = lon // 4
    far = 3 - kind
    mine = lat * 8 + place
    my_row, my_col = mine // 4, lax.rem(mine, 4)
    west = lax.rem(lon + lons - 1, lons)
    east = lax.rem(lon + 1, lons)

    def partner(i):
        return {"lat": i // 8, "lon": lax.rem(i, 8) * 4 + far}

    barrier = pltpu.get_barrier_semaphore()

    def greet(i, carry):
        pl.semaphore_signal(barrier, inc=1, device_id=partner(i), device_id_type=MESH)
        return carry

    lax.fori_loop(0, 32, greet, 0)
    for side in (west, east):
        pl.semaphore_signal(
            barrier, inc=1, device_id={"lat": lat, "lon": side}, device_id_type=MESH
        )

    @pl.when(lat > 0)
    def _():
        for side in (lon, west, east):
            pl.semaphore_signal(
                barrier, inc=1, device_id={"lat": lat - 1, "lon": side}, device_id_type=MESH
            )

    @pl.when(lat < lats - 1)
    def _():
        for side in (lon, west, east):
            pl.semaphore_signal(
                barrier, inc=1, device_id={"lat": lat + 1, "lon": side}, device_id_type=MESH
            )

    for h in range(4):
        masks[h] = pick((16, 128), lambda r, c: c // 32 == h)
    select[...] = pick(
        (256, 256), lambda r, c: r % 128 == (c // 128) * 64 + ((c % 64) // 16) * 16
    )
    ones_bd[...] = pick((256, 256), lambda r, c: (r // 128) * 4 + (r % 64) // 16 == c // 32)
    for r8 in range(8):
        shifts[r8] = pick(
            (64, 208),
            lambda r, c: ((c < 64) & (c + 1 == r))
            | ((c >= 64) & (c < 128) & (c - 64 == r))
            | ((c >= 128) & (c < 192) & (c - 129 == r))
            | ((c == 192 + r8) & (r == 0))
            | ((c == 200 + r8) & (r == 63)),
        )
    for dy in range(3):
        edge_shift[dy] = pick(
            (128, 192),
            lambda r, c: c == ((r // 8) % 2) * 96 + 15 + (r // 16) * 8 + r % 8 + dy,
        )
    perm[...] = pick((256, 256), lambda r, c: (r // 16 == c % 16) & (r % 16 == c // 16))
    for side in range(2):
        first = pick((16, 256), lambda r, c: c == r * 16 + 15 * side)
        for q in range(4):
            x = tokens[16 * q : 16 * q + 16, 48 * side : 48 * side + 16].reshape(256, D)
            edge[side, 16 * q : 16 * q + 16] = dot(first, x).astype(BF16)
    for dy in range(3):
        for dx in range(3):
            dw16[3 * dy + dx] = jnp.broadcast_to(dw_kernel[dy, dx : dx + 1], (16, HID)).astype(BF16)

    def expand_rows(first, count):
        def store(c, v):
            e_mid[pl.ds(first + 1, count), :, c : c + 256] = v.reshape(count, COLS, 256)

        x = tokens[pl.ds(first, count)].reshape(count * COLS, D)
        expand(x, gain_conv[...], w_expand, store)

    def expand_band(band, carry):
        expand_rows(band * 8, 8)
        return carry

    lax.fori_loop(0, 5, expand_band, 0)

    inner = jnp.minimum(lat, 1) + jnp.minimum(lats - 1 - lat, 1)
    pl.semaphore_wait(barrier, 34 + 3 * inner)

    def halo(slot, src, dst, to_lat, to_lon):
        return pltpu.make_async_remote_copy(
            src_ref=src,
            dst_ref=dst,
            send_sem=halo_send.at[slot],
            recv_sem=halo_recv.at[slot],
            device_id={"lat": to_lat, "lon": to_lon},
            device_id_type=MESH,
        )

    to_west = halo(0, edge.at[0], halo_col.at[1, pl.ds(16, 64)], lat, west)
    to_east = halo(1, edge.at[1], halo_col.at[0, pl.ds(16, 64)], lat, east)
    north = [
        halo(2, tokens.at[0], halo_row.at[1], lat - 1, lon),
        halo(3, edge.at[0, pl.ds(0, 16)], halo_col.at[1, pl.ds(80, 16)], lat - 1, west),
        halo(4, edge.at[1, pl.ds(0, 16)], halo_col.at[0, pl.ds(80, 16)], lat - 1, east),
    ]
    south = [
        halo(5, tokens.at[ROWS - 1], halo_row.at[0], lat + 1, lon),
        halo(6, edge.at[0, pl.ds(48, 16)], halo_col.at[1, pl.ds(0, 16)], lat + 1, west),
        halo(7, edge.at[1, pl.ds(48, 16)], halo_col.at[0, pl.ds(0, 16)], lat + 1, east),
    ]
    to_west.start()
    to_east.start()

    @pl.when(lat > 0)
    def _():
        for c in north:
            c.start()

    @pl.when(lat < lats - 1)
    def _():
        for c in south:
            c.start()

    @pl.when(lat == 0)
    def _():
        halo_row[0] = jnp.zeros((COLS, D), BF16)
        halo_col[0, 0:16] = jnp.zeros((16, D), BF16)
        halo_col[1, 0:16] = jnp.zeros((16, D), BF16)

    @pl.when(lat == lats - 1)
    def _():
        halo_row[1] = jnp.zeros((COLS, D), BF16)
        halo_col[0, 80:96] = jnp.zeros((16, D), BF16)
        halo_col[1, 80:96] = jnp.zeros((16, D), BF16)

    lax.fori_loop(5, 8, expand_band, 0)
    spread_bias(bias_in_block, bias_block)
    spread_bias(bias_in_grid, bias_grid)

    to_west.wait()
    to_east.wait()

    @pl.when(lat > 0)
    def _():
        for c in north:
            c.wait_send()
        for c in south:
            c.wait_recv()

    @pl.when(lat < lats - 1)
    def _():
        for c in south:
            c.wait_send()
        for c in north:
            c.wait_recv()

    def store_rows(c, v):
        e_mid[0, :, c : c + 256] = v[0:64]
        e_mid[65, :, c : c + 256] = v[64:128]

    expand(halo_row[...].reshape(2 * COLS, D), gain_conv[...], w_expand, store_rows)

    def store_cols(c, v):
        e_edge[:, c : c + 256] = v

    expand(halo_col[...].reshape(192, D), gain_conv[...], w_expand, store_cols)
    for c in range(0, HID, 256):
        total = jnp.zeros((8, 16, 256), F32)
        for dy in range(3):
            moved = dot(edge_shift[dy], e_edge[:, c : c + 256]).reshape(8, 16, 256)
            west_east = [
                jnp.broadcast_to(dw_kernel[dy, dx : dx + 1, c : c + 256], (8, 256)) for dx in (0, 2)
            ]
            total = total + moved * jnp.concatenate(west_east, axis=0)[None]
        edge_sum[:, :, c : c + 256] = total.astype(BF16)

    def conv_band(band, half):
        first = band * 8

        def row(r, carry):
            for c in range(0, HID, 256):
                parts = []
                e = [e_mid[first + r + dy, :, c : c + 256] for dy in range(3)]
                for dx in range(3):
                    acc = None
                    for dy in range(3):
                        w = dw16[3 * dy + dx, :, c : c + 256]
                        w = jnp.concatenate([w] * 4, axis=0)
                        term = e[dy] * w
                        acc = term if acc is None else acc + term
                    parts.append(acc)
                parts.append(edge_sum[band, :, c : c + 256])
                total = dot(shifts[r], jnp.concatenate(parts, axis=0))
                conv[pl.ds(half * 512 + r * 64, 64), c : c + 256] = gelu(total.astype(BF16))
            return carry

        lax.fori_loop(0, 8, row, 0, unroll=2)

    def pieces(x):
        return jnp.concatenate(
            [x[64 * b + 8 * a : 64 * b + 8 * a + 8] for a in range(8) for b in range(8)], axis=0
        )

    def send(phase):
        def one(i, carry):
            pltpu.make_async_remote_copy(
                src_ref=blocked.at[
                    :, phase * 8 + i // 4, pl.ds(pl.multiple_of(lax.rem(i, 4) * 16, 16), 16), :
                ],
                dst_ref=received.at[phase, lat, :, place],
                send_sem=send_sem.at[phase],
                recv_sem=recv_sem.at[phase],
                device_id=partner(i),
                device_id_type=MESH,
            ).start()
            return carry

        lax.fori_loop(0, 32, one, 0)

    def send_back(phase):
        def one(i, carry):
            pltpu.make_async_remote_copy(
                src_ref=outgoing.at[phase, i // 8, :, lax.rem(i, 8)],
                dst_ref=out.at[
                    :, phase * 8 + my_row, pl.ds(pl.multiple_of(my_col * 16, 16), 16), :
                ],
                send_sem=back_send.at[phase],
                recv_sem=back_recv.at[phase],
                device_id=partner(i),
                device_id_type=MESH,
            ).start()
            return carry

        lax.fori_loop(0, 32, one, 0)

    def conv_and_block(phase):
        def half(i, carry):
            band = i * 4 + phase
            conv_band(band, i)
            x = tokens[pl.ds(band * 8, 8)].reshape(512, D).astype(F32)
            rows = pl.ds(pl.multiple_of(i * 512, 512), 512)
            mixed[rows, :] = pieces(x + dot(conv[rows, :], w_project[...])).astype(BF16)
            return carry

        lax.fori_loop(0, 2, half, 0)
        result = attend(
            mixed, gain_block, qkv_block, bias_block, out_block, masks, select, ones_bd, qkv, att
        )
        result = result + mixed[...].astype(F32)
        for i in range(2):
            blocked[i, pl.ds(phase * 8, 8)] = (
                pieces(result[512 * i : 512 * i + 512]).astype(BF16).reshape(8, 64, D)
            )

    def grid(phase):
        for q in range(4):
            x = received[phase, q].reshape(256, D)
            y = dot(perm[...], x).astype(BF16)
            for p in range(16):
                mixed[64 * p + 16 * q : 64 * p + 16 * q + 16] = y[16 * p : 16 * p + 16]
        result = attend(
            mixed, gain_grid, qkv_grid, bias_grid, out_grid, masks, select, ones_bd, qkv, att
        )
        done = (result + mixed[...].astype(F32)).astype(BF16)
        for q in range(4):
            x = jnp.concatenate(
                [done[64 * p + 16 * q : 64 * p + 16 * q + 16] for p in range(16)], axis=0
            )
            outgoing[phase, q] = dot(perm[...], x).astype(BF16).reshape(2, 8, 16, D)

    def wait_all(ref, sem):
        pltpu.make_async_copy(ref, ref, sem).wait()

    def step(phase, carry):
        @pl.when(phase < PHASES)
        def _():
            conv_and_block(phase)
            send(phase)

        @pl.when(phase > 0)
        def _():
            wait_all(received.at[phase - 1], recv_sem.at[phase - 1])
            grid(phase - 1)
            send_back(phase - 1)

        return carry

    lax.fori_loop(0, PHASES + 1, step, 0)

    def finish(phase, carry):
        wait_all(received.at[phase], send_sem.at[phase])
        wait_all(received.at[phase], back_send.at[phase])
        wait_all(received.at[phase], back_recv.at[phase])
        return carry

    lax.fori_loop(0, PHASES, finish, 0)


def shards(
    tokens,
    gain_conv,
    w_expand,
    dw_kernel,
    w_project,
    gain_block,
    qkv_block,
    bias_block,
    out_block,
    gain_grid,
    qkv_grid,
    bias_grid,
    out_grid,
):
    operands = [
        tokens,
        gain_conv.reshape(1, D),
        w_expand,
        dw_kernel,
        w_project,
        gain_block.reshape(1, D),
        qkv_block,
        bias_block,
        out_block,
        gain_grid.reshape(1, D),
        qkv_grid,
        bias_grid,
        out_grid,
    ]
    result = pl.pallas_call(
        kernel,
        out_shape=jax.ShapeDtypeStruct((2, 32, COLS, D), BF16),
        in_specs=[pl.BlockSpec(memory_space=pltpu.VMEM)] * len(operands),
        out_specs=pl.BlockSpec(memory_space=pltpu.VMEM),
        scratch_shapes=[
            pltpu.VMEM((66, COLS, HID), BF16),
            pltpu.VMEM((192, HID), BF16),
            pltpu.VMEM((2, COLS, D), BF16),
            pltpu.VMEM((2, 96, D), BF16),
            pltpu.VMEM((2, 64, D), BF16),
            pltpu.VMEM((8, 16, HID), BF16),
            pltpu.VMEM((9, 16, HID), BF16),
            pltpu.VMEM((64, 512), F32),
            pltpu.VMEM((64, 512), F32),
            pltpu.VMEM((4, 16, 128), BF16),
            pltpu.VMEM((256, 256), BF16),
            pltpu.VMEM((256, 256), BF16),
            pltpu.VMEM((8, 64, 208), BF16),
            pltpu.VMEM((3, 128, 192), BF16),
            pltpu.VMEM((256, 256), BF16),
            pltpu.VMEM((1024, HID), BF16),
            pltpu.VMEM((1024, D), BF16),
            pltpu.VMEM((1024, 3 * D), BF16),
            pltpu.VMEM((1024, D), BF16),
            pltpu.VMEM((2, 32, COLS, D), BF16),
            pltpu.VMEM((PHASES, 4, 2, 8, 16, D), BF16),
            pltpu.VMEM((PHASES, 4, 2, 8, 16, D), BF16),
            pltpu.SemaphoreType.DMA((8,)),
            pltpu.SemaphoreType.DMA((8,)),
            pltpu.SemaphoreType.DMA((PHASES,)),
            pltpu.SemaphoreType.DMA((PHASES,)),
            pltpu.SemaphoreType.DMA((PHASES,)),
            pltpu.SemaphoreType.DMA((PHASES,)),
        ],
        compiler_params=pltpu.CompilerParams(
            collective_id=0, has_side_effects=True, vmem_limit_bytes=60 * 1024 * 1024
        ),
    )(*operands)
    return result.reshape(ROWS, COLS, D)


def solution(mesh):
    placed = (P("lat", "lon", None), P(), P(), P(), P(), P(), P(), P(), P(), P(), P(), P(), P())
    return jax.shard_map(
        shards, mesh=mesh, in_specs=placed, out_specs=P("lat", "lon", None), check_vma=False
    )
```

time: 110 us -> 86.5 us (0.79)
  Pallas kernels: 98.4 us -> 83.2 us
  local copies, waits for them, and re-layouts: 10.7 us -> 3.16 us
    pallas_call x1, Pallas kernels: 98.4 us -> 83.2 us  [shards(): pl.pallas_call(kernel, out_shape=jax.ShapeDtypeStruct((2, 32, COLS, D), B...]
    reshape x3 -> x0, local copies, waits for them, and re-layouts: 2.24 us -> none  [the longest x2 1.54 us: spread_bias(): (bias * LOG2E).reshape(HEADS, 64, 4, 16).transpose(1, 2, 0, 3)]
    slice x2 -> x0, local copies, waits for them, and re-layouts: 2.02 us -> none  [the longest x1 1.14 us: shards(): tokens[:, COLS - 1]]
    unnamed x5 -> x1, local copies, waits for them, and re-layouts: 4.37 us -> 3.16 us
where the time goes in v3:
time: 86.5 us; the launch traced here: 86.4 us
  Pallas kernels  83.2 us (96%)
  local copies, waits for them, and re-layouts  3.16 us (4%)
    pallas_call x1, Pallas kernels, shards(): pl.pallas_call(kernel, out_shape=jax.ShapeDtypeStruct((2, 32, COLS, D), B...  83.2 us
    unnamed x1, local copies, waits for them, and re-layouts  3.16 us

profile of v3, /device:TPU:1, one launch (start us, length us, event | category | flops | bytes accessed | tf_op | source)
XLA Modules:
  0.0 86.4 jit_solution(16446616434639017597)
XLA Ops:
  0.0 83.2 %shard_map.127 = bf16[2,32,64,256]{3,2,1,0:T(8,128)(2,1)} custom-call(bf16[64,64,256]{2,1,0:T(8,128)(2,1)} %tokens.1, f32[1,256]{1,0:T(1,128)} %bitcast.5, bf16[256,1024]{1,0:T(8,128)(2,1)} %w_expand.1, f32[3,3,1024]{2,1,0:T(4,128)} %dw_kernel.1, bf16[1024,256]{1,0:T(8,128)(2,1)} %w_project.1, f32[1,256]{1,0:T(1,128)} %bitcast.6, ...), custom_call_target="tpu_custom_call" | custom-call | tf_op jit(solution)/shard_map/pallas_call | solution.py:514
  83.2 3.2 %copy.15 = bf16[64,64,256]{2,1,0:T(8,128)(2,1)} copy(bf16[64,64,256]{2,1,0:T(8,128)(2,1)} %bitcast.4) | data formatting | bytes 4194304

commit v4 on v3

--- a/solution.py
+++ b/solution.py
@@ -68,10 +68,10 @@
     qkv[:, 0:256] = (dot(n, w_qkv[:, 0:256]) * scale).astype(BF16)
     qkv[:, 256:512] = dot(n, w_qkv[:, 256:512]).astype(BF16)
     qkv[:, 512:768] = dot(n, w_qkv[:, 512:768]).astype(BF16)
-    size = BATCH * 64
+    size = min(BATCH * 64, x_ref.shape[0])
 
     def batch(first):
-        rows = [pl.ds(first + i * 64, 64) for i in range(BATCH)]
+        rows = [pl.ds(first + i * 64, 64) for i in range(size // 64)]
         scores = [
             jnp.concatenate(
                 [
@@ -141,19 +141,19 @@
 
 
 def kernel(
-    tokens,
-    gain_conv,
-    w_expand,
-    dw_kernel,
-    w_project,
-    gain_block,
-    qkv_block,
-    bias_in_block,
-    out_block,
-    gain_grid,
-    qkv_grid,
-    bias_in_grid,
-    out_grid,
+    tokens_hbm,
+    gain_conv_hbm,
+    w_expand_hbm,
+    dw_kernel_hbm,
+    w_project_hbm,
+    gain_block_hbm,
+    qkv_block_hbm,
+    bias_in_block_hbm,
+    out_block_hbm,
+    gain_grid_hbm,
+    qkv_grid_hbm,
+    bias_in_grid_hbm,
+    out_grid_hbm,
     out,
     e_mid,
     e_edge,
@@ -183,6 +183,20 @@
     recv_sem,
     back_send,
     back_recv,
+    tokens,
+    gain_conv,
+    w_expand,
+    dw_kernel,
+    w_project,
+    gain_block,
+    qkv_block,
+    bias_in_block,
+    out_block,
+    gain_grid,
+    qkv_grid,
+    bias_in_grid,
+    out_grid,
+    fetch_sem,
 ):
     lat = lax.axis_index("lat")
     lon = lax.axis_index("lon")
@@ -199,6 +213,29 @@
     def partner(i):
         return {"lat": i // 8, "lon": lax.rem(i, 8) * 4 + far}
 
+    fetched = [
+        pltpu.make_async_copy(src, dst, fetch_sem.at[i])
+        for i, (src, dst) in enumerate(
+            [
+                (tokens_hbm, tokens),
+                (w_expand_hbm, w_expand),
+                (gain_conv_hbm, gain_conv),
+                (dw_kernel_hbm, dw_kernel),
+                (bias_in_block_hbm, bias_in_block),
+                (bias_in_grid_hbm, bias_in_grid),
+                (w_project_hbm, w_project),
+                (gain_block_hbm, gain_block),
+                (qkv_block_hbm, qkv_block),
+                (out_block_hbm, out_block),
+                (gain_grid_hbm, gain_grid),
+                (qkv_grid_hbm, qkv_grid),
+                (out_grid_hbm, out_grid),
+            ]
+        )
+    ]
+    for copy in fetched:
+        copy.start()
+
     barrier = pltpu.get_barrier_semaphore()
 
     def greet(i, carry):
@@ -225,6 +262,76 @@
                 barrier, inc=1, device_id={"lat": lat + 1, "lon": side}, device_id_type=MESH
             )
 
+    for copy in fetched[:3]:
+        copy.wait()
+    for side in range(2):
+        first = pick((16, 256), lambda r, c: c == r * 16 + 15 * side)
+        for q in range(4):
+            x = tokens[16 * q : 16 * q + 16, 48 * side : 48 * side + 16].reshape(256, D)
+            edge[side, 16 * q : 16 * q + 16] = dot(first, x).astype(BF16)
+
+    def expand_rows(first, count):
+        def store(c, v):
+            e_mid[pl.ds(first + 1, count), :, c : c + 256] = v.reshape(count, COLS, 256)
+
+        x = tokens[pl.ds(first, count)].reshape(count * COLS, D)
+        expand(x, gain_conv[...], w_expand, store)
+
+    expand_rows(0, 9)
+
+    inner = jnp.minimum(lat, 1) + jnp.minimum(lats - 1 - lat, 1)
+    pl.semaphore_wait(barrier, 34 + 3 * inner)
+
+    def halo(slot, src, dst, to_lat, to_lon):
+        return pltpu.make_async_remote_copy(
+            src_ref=src,
+            dst_ref=dst,
+            send_sem=halo_send.at[slot],
+            recv_sem=halo_recv.at[slot],
+            device_id={"lat": to_lat, "lon": to_lon},
+            device_id_type=MESH,
+        )
+
+    to_west = halo(0, edge.at[0], halo_col.at[1, pl.ds(16, 64)], lat, west)
+    to_east = halo(1, edge.at[1], halo_col.at[0, pl.ds(16, 64)], lat, east)
+    north = [
+        halo(2, tokens.at[0], halo_row.at[1], lat - 1, lon),
+        halo(3, edge.at[0, pl.ds(0, 16)], halo_col.at[1, pl.ds(80, 16)], lat - 1, west),
+        halo(4, edge.at[1, pl.ds(0, 16)], halo_col.at[0, pl.ds(80, 16)], lat - 1, east),
+    ]
+    south = [
+        halo(5, tokens.at[ROWS - 1], halo_row.at[0], lat + 1, lon),
+        halo(6, edge.at[0, pl.ds(48, 16)], halo_col.at[1, pl.ds(0, 16)], lat + 1, west),
+        halo(7, edge.at[1, pl.ds(48, 16)], halo_col.at[0, pl.ds(0, 16)], lat + 1, east),
+    ]
+    to_west.start()
+    to_east.start()
+
+    @pl.when(lat > 0)
+    def _():
+        for c in north:
+            c.start()
+
+    @pl.when(lat < lats - 1)
+    def _():
+        for c in south:
+            c.start()
+
+    @pl.when(lat == 0)
+    def _():
+        halo_row[0] = jnp.zeros((COLS, D), BF16)
+        halo_col[0, 0:16] = jnp.zeros((16, D), BF16)
+        halo_col[1, 0:16] = jnp.zeros((16, D), BF16)
+
+    @pl.when(lat == lats - 1)
+    def _():
+        halo_row[1] = jnp.zeros((COLS, D), BF16)
+        halo_col[0, 80:96] = jnp.zeros((16, D), BF16)
+        halo_col[1, 80:96] = jnp.zeros((16, D), BF16)
+
+    expand_rows(31, 10)
+    for copy in fetched[3:]:
+        copy.wait()
     for h in range(4):
         masks[h] = pick((16, 128), lambda r, c: c // 32 == h)
     select[...] = pick(
@@ -246,79 +353,10 @@
             lambda r, c: c == ((r // 8) % 2) * 96 + 15 + (r // 16) * 8 + r % 8 + dy,
         )
     perm[...] = pick((256, 256), lambda r, c: (r // 16 == c % 16) & (r % 16 == c // 16))
-    for side in range(2):
-        first = pick((16, 256), lambda r, c: c == r * 16 + 15 * side)
-        for q in range(4):
-            x = tokens[16 * q : 16 * q + 16, 48 * side : 48 * side + 16].reshape(256, D)
-            edge[side, 16 * q : 16 * q + 16] = dot(first, x).astype(BF16)
     for dy in range(3):
         for dx in range(3):
             dw16[3 * dy + dx] = jnp.broadcast_to(dw_kernel[dy, dx : dx + 1], (16, HID)).astype(BF16)
 
-    def expand_rows(first, count):
-        def store(c, v):
-            e_mid[pl.ds(first + 1, count), :, c : c + 256] = v.reshape(count, COLS, 256)
-
-        x = tokens[pl.ds(first, count)].reshape(count * COLS, D)
-        expand(x, gain_conv[...], w_expand, store)
-
-    def expand_band(band, carry):
-        expand_rows(band * 8, 8)
-        return carry
-
-    lax.fori_loop(0, 5, expand_band, 0)
-
-    inner = jnp.minimum(lat, 1) + jnp.minimum(lats - 1 - lat, 1)
-    pl.semaphore_wait(barrier, 34 + 3 * inner)
-
-    def halo(slot, src, dst, to_lat, to_lon):
-        return pltpu.make_async_remote_copy(
-            src_ref=src,
-            dst_ref=dst,
-            send_sem=halo_send.at[slot],
-            recv_sem=halo_recv.at[slot],
-            device_id={"lat": to_lat, "lon": to_lon},
-            device_id_type=MESH,
-        )
-
-    to_west = halo(0, edge.at[0], halo_col.at[1, pl.ds(16, 64)], lat, west)
-    to_east = halo(1, edge.at[1], halo_col.at[0, pl.ds(16, 64)], lat, east)
-    north = [
-        halo(2, tokens.at[0], halo_row.at[1], lat - 1, lon),
-        halo(3, edge.at[0, pl.ds(0, 16)], halo_col.at[1, pl.ds(80, 16)], lat - 1, west),
-        halo(4, edge.at[1, pl.ds(0, 16)], halo_col.at[0, pl.ds(80, 16)], lat - 1, east),
-    ]
-    south = [
-        halo(5, tokens.at[ROWS - 1], halo_row.at[0], lat + 1, lon),
-        halo(6, edge.at[0, pl.ds(48, 16)], halo_col.at[1, pl.ds(0, 16)], lat + 1, west),
-        halo(7, edge.at[1, pl.ds(48, 16)], halo_col.at[0, pl.ds(0, 16)], lat + 1, east),
-    ]
-    to_west.start()
-    to_east.start()
-
-    @pl.when(lat > 0)
-    def _():
-        for c in north:
-            c.start()
-
-    @pl.when(lat < lats - 1)
-    def _():
-        for c in south:
-            c.start()
-
-    @pl.when(lat == 0)
-    def _():
-        halo_row[0] = jnp.zeros((COLS, D), BF16)
-        halo_col[0, 0:16] = jnp.zeros((16, D), BF16)
-        halo_col[1, 0:16] = jnp.zeros((16, D), BF16)
-
-    @pl.when(lat == lats - 1)
-    def _():
-        halo_row[1] = jnp.zeros((COLS, D), BF16)
-        halo_col[0, 80:96] = jnp.zeros((16, D), BF16)
-        halo_col[1, 80:96] = jnp.zeros((16, D), BF16)
-
-    lax.fori_loop(5, 8, expand_band, 0)
     spread_bias(bias_in_block, bias_block)
     spread_bias(bias_in_grid, bias_grid)
 
@@ -359,7 +397,7 @@
             total = total + moved * jnp.concatenate(west_east, axis=0)[None]
         edge_sum[:, :, c : c + 256] = total.astype(BF16)
 
-    def conv_band(band, half):
+    def conv_band(band):
         first = band * 8
 
         def row(r, carry):
@@ -376,23 +414,23 @@
                     parts.append(acc)
                 parts.append(edge_sum[band, :, c : c + 256])
                 total = dot(shifts[r], jnp.concatenate(parts, axis=0))
-                conv[pl.ds(half * 512 + r * 64, 64), c : c + 256] = gelu(total.astype(BF16))
+                conv[pl.ds(r * 64, 64), c : c + 256] = gelu(total.astype(BF16))
             return carry
 
-        lax.fori_loop(0, 8, row, 0, unroll=2)
+        lax.fori_loop(0, 8, row, 0, unroll=4)
 
     def pieces(x):
         return jnp.concatenate(
             [x[64 * b + 8 * a : 64 * b + 8 * a + 8] for a in range(8) for b in range(8)], axis=0
         )
 
-    def send(phase):
+    def send(phase, half):
         def one(i, carry):
             pltpu.make_async_remote_copy(
                 src_ref=blocked.at[
-                    :, phase * 8 + i // 4, pl.ds(pl.multiple_of(lax.rem(i, 4) * 16, 16), 16), :
+                    half, phase * 8 + i // 4, pl.ds(pl.multiple_of(lax.rem(i, 4) * 16, 16), 16), :
                 ],
-                dst_ref=received.at[phase, lat, :, place],
+                dst_ref=received.at[phase, lat, half, place],
                 send_sem=send_sem.at[phase],
                 recv_sem=recv_sem.at[phase],
                 device_id=partner(i),
@@ -400,7 +438,7 @@
             ).start()
             return carry
 
-        lax.fori_loop(0, 32, one, 0)
+        lax.fori_loop(0, 32, one, 0, unroll=True)
 
     def send_back(phase):
         def one(i, carry):
@@ -416,26 +454,36 @@
             ).start()
             return carry
 
-        lax.fori_loop(0, 32, one, 0)
+        lax.fori_loop(0, 32, one, 0, unroll=True)
 
     def conv_and_block(phase):
         def half(i, carry):
             band = i * 4 + phase
-            conv_band(band, i)
-            x = tokens[pl.ds(band * 8, 8)].reshape(512, D).astype(F32)
-            rows = pl.ds(pl.multiple_of(i * 512, 512), 512)
-            mixed[rows, :] = pieces(x + dot(conv[rows, :], w_project[...])).astype(BF16)
+            first = band * 8
+
+            @pl.when((phase > 0) & (band < 7))
+            def _():
+                expand_rows(first + 1, 8)
+
+            @pl.when(band == 7)
+            def _():
+                expand_rows(first + 1, 7)
+
+            conv_band(band)
+            x = tokens[pl.ds(first, 8)].reshape(512, D).astype(F32)
+            x = pieces(x + dot(conv[0:512, :], w_project[...])).astype(BF16)
+            mixed[0:512, :] = x
+            result = attend(
+                mixed.at[0:512], gain_block, qkv_block, bias_block, out_block, masks, select,
+                ones_bd, qkv.at[0:512], att.at[0:512],
+            )
+            blocked[i, pl.ds(phase * 8, 8)] = (
+                pieces(result + x.astype(F32)).astype(BF16).reshape(8, 64, D)
+            )
+            send(phase, i)
             return carry
 
         lax.fori_loop(0, 2, half, 0)
-        result = attend(
-            mixed, gain_block, qkv_block, bias_block, out_block, masks, select, ones_bd, qkv, att
-        )
-        result = result + mixed[...].astype(F32)
-        for i in range(2):
-            blocked[i, pl.ds(phase * 8, 8)] = (
-                pieces(result[512 * i : 512 * i + 512]).astype(BF16).reshape(8, 64, D)
-            )
 
     def grid(phase):
         for q in range(4):
@@ -460,7 +508,6 @@
         @pl.when(phase < PHASES)
         def _():
             conv_and_block(phase)
-            send(phase)
 
         @pl.when(phase > 0)
         def _():
@@ -479,6 +526,17 @@
         return carry
 
     lax.fori_loop(0, PHASES, finish, 0)
+
+
+def copy_kernel(source, target, sem):
+    parts = [
+        pltpu.make_async_copy(source.at[pl.ds(8 * i, 8)], target.at[pl.ds(8 * i, 8)], sem.at[i])
+        for i in range(8)
+    ]
+    for part in parts:
+        part.start()
+    for part in parts:
+        part.wait()
 
 
 def shards(
@@ -514,8 +572,8 @@
     result = pl.pallas_call(
         kernel,
         out_shape=jax.ShapeDtypeStruct((2, 32, COLS, D), BF16),
-        in_specs=[pl.BlockSpec(memory_space=pltpu.VMEM)] * len(operands),
-        out_specs=pl.BlockSpec(memory_space=pltpu.VMEM),
+        in_specs=[pl.BlockSpec(memory_space=pl.ANY)] * len(operands),
+        out_specs=pl.BlockSpec(memory_space=pl.ANY),
         scratch_shapes=[
             pltpu.VMEM((66, COLS, HID), BF16),
             pltpu.VMEM((192, HID), BF16),
@@ -532,7 +590,7 @@
             pltpu.VMEM((8, 64, 208), BF16),
             pltpu.VMEM((3, 128, 192), BF16),
             pltpu.VMEM((256, 256), BF16),
-            pltpu.VMEM((1024, HID), BF16),
+            pltpu.VMEM((512, HID), BF16),
             pltpu.VMEM((1024, D), BF16),
             pltpu.VMEM((1024, 3 * D), BF16),
             pltpu.VMEM((1024, D), BF16),
@@ -545,12 +603,21 @@
             pltpu.SemaphoreType.DMA((PHASES,)),
             pltpu.SemaphoreType.DMA((PHASES,)),
             pltpu.SemaphoreType.DMA((PHASES,)),
+            *[pltpu.VMEM(a.shape, a.dtype) for a in operands],
+            pltpu.SemaphoreType.DMA((len(operands),)),
         ],
         compiler_params=pltpu.CompilerParams(
             collective_id=0, has_side_effects=True, vmem_limit_bytes=60 * 1024 * 1024
         ),
     )(*operands)
-    return result.reshape(ROWS, COLS, D)
+    result = result.reshape(ROWS, COLS, D)
+    return pl.pallas_call(
+        copy_kernel,
+        out_shape=jax.ShapeDtypeStruct(result.shape, result.dtype),
+        in_specs=[pl.BlockSpec(memory_space=pl.ANY)],
+        out_specs=pl.BlockSpec(memory_space=pl.ANY),
+        scratch_shapes=[pltpu.SemaphoreType.DMA((8,))],
+    )(result)
 
 
 def solution(mesh):

time: 86.5 us -> 147 us (1.70)
  Pallas kernels: 83.2 us -> 147 us
  local copies, waits for them, and re-layouts: 3.16 us -> 0 us
    pallas_call x0 -> x1, Pallas kernels: none -> 64.7 us  [shards(): pl.pallas_call(copy_kernel, out_shape=jax.ShapeDtypeStruct(result.shape,...]
    unnamed x1 -> x0, local copies, waits for them, and re-layouts: 3.16 us -> none
where the time goes in v4:
time: 147 us
  Pallas kernels  147 us (100%)
    pallas_call x1, Pallas kernels, shards(): pl.pallas_call(kernel, out_shape=jax.ShapeDtypeStruct((2, 32, COLS, D), B...  81.8 us
    pallas_call x1, Pallas kernels, shards(): pl.pallas_call(copy_kernel, out_shape=jax.ShapeDtypeStruct(result.shape,...  64.7 us

profile of v4, /device:TPU:1, one launch (start us, length us, event | category | flops | bytes accessed | tf_op | source)
XLA Modules:
  0.0 146.5 jit_solution(6372500236134372752)
XLA Ops:
  0.0 81.8 %shard_map.127 = bf16[2,32,64,256]{3,2,1,0:T(8,128)(2,1)} custom-call(bf16[64,64,256]{2,1,0:T(8,128)(2,1)} %tokens_hbm.1, f32[1,256]{1,0:T(1,128)} %bitcast.5, bf16[256,1024]{1,0:T(8,128)(2,1)} %w_expand_hbm.1, f32[3,3,1024]{2,1,0:T(4,128)} %dw_kernel_hbm.1, bf16[1024,256]{1,0:T(8,128)(2,1)} %w_project_hbm.1, f32[1,256]{1,0:T(1,128)} %bitcast.6, ...), custom_call_target="tpu_custom_call" | custom-call | tf_op jit(solution)/shard_map/pallas_call | solution.py:572
  81.8 64.7 %shard_map.128 = bf16[64,64,256]{2,1,0:T(8,128)(2,1)} custom-call(bf16[64,64,256]{2,1,0:T(8,128)(2,1)} %bitcast.4), custom_call_target="tpu_custom_call" | custom-call | tf_op jit(solution)/shard_map/pallas_call | solution.py:614

commit v5 on v4

--- a/solution.py
+++ b/solution.py
@@ -32,15 +32,15 @@
     return half + half * jnp.tanh(inner)
 
 
-def norm(x, gain):
+def norm(x, gain, average):
     xf = x.astype(F32)
     d = xf - jnp.mean(xf, axis=-1, keepdims=True)
-    var = jnp.mean(d * d, axis=-1, keepdims=True)
+    var = dot((d * d).astype(BF16), average)
     return (d * lax.rsqrt(var + 1e-05) * gain).astype(BF16)
 
 
-def expand(x, gain, w_expand, store):
-    n = norm(x, gain)
+def expand(x, gain, average, w_expand, store):
+    n = norm(x, gain, average)
     for c in range(0, HID, 256):
         store(c, gelu(dot(n, w_expand[:, c : c + 256]).astype(BF16)))
 
@@ -62,8 +62,8 @@
     return dot(jnp.concatenate([high, low], axis=1), select[...])
 
 
-def attend(x_ref, gain, w_qkv, bias, w_out, masks, select, ones_bd, qkv, mixed):
-    n = norm(x_ref[...], gain[...])
+def attend(x_ref, gain, average, w_qkv, bias, w_out, masks, select, ones_bd, qkv, mixed):
+    n = norm(x_ref[...], gain[...], average[...])
     scale = LOG2E / 32**0.5
     qkv[:, 0:256] = (dot(n, w_qkv[:, 0:256]) * scale).astype(BF16)
     qkv[:, 256:512] = dot(n, w_qkv[:, 256:512]).astype(BF16)
@@ -130,7 +130,7 @@
                 for h in range(4):
                     at, to = (2 * tile + k) * 16, k * 64 + h * 16
                     moved = pltpu.roll(twice[h], (to - at) % 128, 1)
-                    acc = jnp.where(lane // 16 == to // 16, moved, acc)
+                    acc = jnp.where((lane >> 4) == to // 16, moved, acc)
             target[:, 256 * u + 128 * tile : 256 * u + 128 * tile + 128] = acc
 
 
@@ -164,6 +164,7 @@
     dw16,
     bias_block,
     bias_grid,
+    average,
     masks,
     select,
     ones_bd,
@@ -262,6 +263,7 @@
                 barrier, inc=1, device_id={"lat": lat + 1, "lon": side}, device_id_type=MESH
             )
 
+    average[...] = jnp.full((D, D), 1.0 / D, BF16)
     for copy in fetched[:3]:
         copy.wait()
     for side in range(2):
@@ -275,7 +277,7 @@
             e_mid[pl.ds(first + 1, count), :, c : c + 256] = v.reshape(count, COLS, 256)
 
         x = tokens[pl.ds(first, count)].reshape(count * COLS, D)
-        expand(x, gain_conv[...], w_expand, store)
+        expand(x, gain_conv[...], average[...], w_expand, store)
 
     expand_rows(0, 9)
 
@@ -333,26 +335,24 @@
     for copy in fetched[3:]:
         copy.wait()
     for h in range(4):
-        masks[h] = pick((16, 128), lambda r, c: c // 32 == h)
+        masks[h] = pick((16, 128), lambda r, c: (c >> 5) == h)
     select[...] = pick(
-        (256, 256), lambda r, c: r % 128 == (c // 128) * 64 + ((c % 64) // 16) * 16
+        (256, 256), lambda r, c: (r & 127) == (c >> 7) * 64 + (c & 48)
     )
-    ones_bd[...] = pick((256, 256), lambda r, c: (r // 128) * 4 + (r % 64) // 16 == c // 32)
+    ones_bd[...] = pick((256, 256), lambda r, c: (r >> 7) * 64 + (r & 48) == (c >> 5) << 4)
     for r8 in range(8):
         shifts[r8] = pick(
             (64, 208),
-            lambda r, c: ((c < 64) & (c + 1 == r))
-            | ((c >= 64) & (c < 128) & (c - 64 == r))
-            | ((c >= 128) & (c < 192) & (c - 129 == r))
+            lambda r, c: ((c < 192) & ((c & 63) + 1 - (c >> 6) == r))
             | ((c == 192 + r8) & (r == 0))
             | ((c == 200 + r8) & (r == 63)),
         )
     for dy in range(3):
         edge_shift[dy] = pick(
             (128, 192),
-            lambda r, c: c == ((r // 8) % 2) * 96 + 15 + (r // 16) * 8 + r % 8 + dy,
-        )
-    perm[...] = pick((256, 256), lambda r, c: (r // 16 == c % 16) & (r % 16 == c // 16))
+            lambda r, c: c == ((r >> 3) & 1) * 96 + 15 + (r >> 4) * 8 + (r & 7) + dy,
+        )
+    perm[...] = pick((256, 256), lambda r, c: r == ((c & 15) << 4) + (c >> 4))
     for dy in range(3):
         for dx in range(3):
             dw16[3 * dy + dx] = jnp.broadcast_to(dw_kernel[dy, dx : dx + 1], (16, HID)).astype(BF16)
@@ -381,12 +381,12 @@
         e_mid[0, :, c : c + 256] = v[0:64]
         e_mid[65, :, c : c + 256] = v[64:128]
 
-    expand(halo_row[...].reshape(2 * COLS, D), gain_conv[...], w_expand, store_rows)
+    expand(halo_row[...].reshape(2 * COLS, D), gain_conv[...], average[...], w_expand, store_rows)
 
     def store_cols(c, v):
         e_edge[:, c : c + 256] = v
 
-    expand(halo_col[...].reshape(192, D), gain_conv[...], w_expand, store_cols)
+    expand(halo_col[...].reshape(192, D), gain_conv[...], average[...], w_expand, store_cols)
     for c in range(0, HID, 256):
         total = jnp.zeros((8, 16, 256), F32)
         for dy in range(3):
@@ -474,7 +474,7 @@
             x = pieces(x + dot(conv[0:512, :], w_project[...])).astype(BF16)
             mixed[0:512, :] = x
             result = attend(
-                mixed.at[0:512], gain_block, qkv_block, bias_block, out_block, masks, select,
+                mixed.at[0:512], gain_block, average, qkv_block, bias_block, out_block, masks, select,
                 ones_bd, qkv.at[0:512], att.at[0:512],
             )
             blocked[i, pl.ds(phase * 8, 8)] = (
@@ -492,7 +492,7 @@
             for p in range(16):
                 mixed[64 * p + 16 * q : 64 * p + 16 * q + 16] = y[16 * p : 16 * p + 16]
         result = attend(
-            mixed, gain_grid, qkv_grid, bias_grid, out_grid, masks, select, ones_bd, qkv, att
+            mixed, gain_grid, average, qkv_grid, bias_grid, out_grid, masks, select, ones_bd, qkv, att
         )
         done = (result + mixed[...].astype(F32)).astype(BF16)
         for q in range(4):
@@ -528,15 +528,21 @@
     lax.fori_loop(0, PHASES, finish, 0)
 
 
-def copy_kernel(source, target, sem):
-    parts = [
-        pltpu.make_async_copy(source.at[pl.ds(8 * i, 8)], target.at[pl.ds(8 * i, 8)], sem.at[i])
-        for i in range(8)
+def copy_kernel(source, target, held, sem_in, sem_out):
+    parts = [pl.ds(8 * i, 8) for i in range(8)]
+    loads = [
+        pltpu.make_async_copy(source.at[p], held.at[p], sem_in.at[i]) for i, p in enumerate(parts)
     ]
-    for part in parts:
-        part.start()
-    for part in parts:
-        part.wait()
+    stores = [
+        pltpu.make_async_copy(held.at[p], target.at[p], sem_out.at[i]) for i, p in enumerate(parts)
+    ]
+    for load in loads:
+        load.start()
+    for load, store in zip(loads, stores):
+        load.wait()
+        store.start()
+    for store in stores:
+        store.wait()
 
 
 def shards(
@@ -584,6 +590,7 @@
             pltpu.VMEM((9, 16, HID), BF16),
             pltpu.VMEM((64, 512), F32),
             pltpu.VMEM((64, 512), F32),
+            pltpu.VMEM((D, D), BF16),
             pltpu.VMEM((4, 16, 128), BF16),
             pltpu.VMEM((256, 256), BF16),
             pltpu.VMEM((256, 256), BF16),
@@ -616,7 +623,11 @@
         out_shape=jax.ShapeDtypeStruct(result.shape, result.dtype),
         in_specs=[pl.BlockSpec(memory_space=pl.ANY)],
         out_specs=pl.BlockSpec(memory_space=pl.ANY),
-        scratch_shapes=[pltpu.SemaphoreType.DMA((8,))],
+        scratch_shapes=[
+            pltpu.VMEM(result.shape, result.dtype),
+            pltpu.SemaphoreType.DMA((8,)),
+            pltpu.SemaphoreType.DMA((8,)),
+        ],
     )(result)
 
 

time: 147 us -> 82.9 us (0.56)
  Pallas kernels: 147 us -> 82.7 us
    pallas_call x1, Pallas kernels: 64.7 us -> 2.39 us  [shards(): pl.pallas_call(copy_kernel, out_shape=jax.ShapeDtypeStruct(result.shape,...]
    pallas_call x1, Pallas kernels: 81.8 us -> 80.3 us  [shards(): pl.pallas_call(kernel, out_shape=jax.ShapeDtypeStruct((2, 32, COLS, D), B...]
where the time goes in v5:
time: 82.9 us; the launch traced here: 82.7 us
  Pallas kernels  82.7 us (100%)
    pallas_call x1, Pallas kernels, shards(): pl.pallas_call(kernel, out_shape=jax.ShapeDtypeStruct((2, 32, COLS, D), B...  80.3 us
    pallas_call x1, Pallas kernels, shards(): pl.pallas_call(copy_kernel, out_shape=jax.ShapeDtypeStruct(result.shape,...  2.39 us

profile of v5, /device:TPU:1, one launch (start us, length us, event | category | flops | bytes accessed | tf_op | source)
XLA Modules:
  0.0 82.7 jit_solution(6464414782430622989)
XLA Ops:
  0.0 80.3 %shard_map.127 = bf16[2,32,64,256]{3,2,1,0:T(8,128)(2,1)} custom-call(bf16[64,64,256]{2,1,0:T(8,128)(2,1)} %tokens_hbm.1, f32[1,256]{1,0:T(1,128)} %bitcast.5, bf16[256,1024]{1,0:T(8,128)(2,1)} %w_expand_hbm.1, f32[3,3,1024]{2,1,0:T(4,128)} %dw_kernel_hbm.1, bf16[1024,256]{1,0:T(8,128)(2,1)} %w_project_hbm.1, f32[1,256]{1,0:T(1,128)} %bitcast.6, ...), custom_call_target="tpu_custom_call" | custom-call | tf_op jit(solution)/shard_map/pallas_call | solution.py:578
  80.3 2.4 %shard_map.128 = bf16[64,64,256]{2,1,0:T(8,128)(2,1)} custom-call(bf16[64,64,256]{2,1,0:T(8,128)(2,1)} %bitcast.4), custom_call_target="tpu_custom_call" | custom-call | tf_op jit(solution)/shard_map/pallas_call | solution.py:621

commit v6 on v5

--- a/solution.py
+++ b/solution.py
@@ -10,6 +10,7 @@
 F32 = jnp.float32
 ROWS, COLS, D, HID, HEADS = 64, 64, 256, 1024, 8
 PHASES = 4
+EARLY = 5
 BATCH = 16
 LOG2E = 1.4426950408889634
 
@@ -243,7 +244,7 @@
         pl.semaphore_signal(barrier, inc=1, device_id=partner(i), device_id_type=MESH)
         return carry
 
-    lax.fori_loop(0, 32, greet, 0)
+    lax.fori_loop(0, 32, greet, 0, unroll=True)
     for side in (west, east):
         pl.semaphore_signal(
             barrier, inc=1, device_id={"lat": lat, "lon": side}, device_id_type=MESH
@@ -279,7 +280,11 @@
         x = tokens[pl.ds(first, count)].reshape(count * COLS, D)
         expand(x, gain_conv[...], average[...], w_expand, store)
 
-    expand_rows(0, 9)
+    def expand_band(band, carry):
+        expand_rows(band * 8, 8)
+        return carry
+
+    lax.fori_loop(0, EARLY, expand_band, 0)
 
     inner = jnp.minimum(lat, 1) + jnp.minimum(lats - 1 - lat, 1)
     pl.semaphore_wait(barrier, 34 + 3 * inner)
@@ -331,7 +336,7 @@
         halo_col[0, 80:96] = jnp.zeros((16, D), BF16)
         halo_col[1, 80:96] = jnp.zeros((16, D), BF16)
 
-    expand_rows(31, 10)
+    lax.fori_loop(EARLY, 8, expand_band, 0)
     for copy in fetched[3:]:
         copy.wait()
     for h in range(4):
@@ -460,14 +465,6 @@
         def half(i, carry):
             band = i * 4 + phase
             first = band * 8
-
-            @pl.when((phase > 0) & (band < 7))
-            def _():
-                expand_rows(first + 1, 8)
-
-            @pl.when(band == 7)
-            def _():
-                expand_rows(first + 1, 7)
 
             conv_band(band)
             x = tokens[pl.ds(first, 8)].reshape(512, D).astype(F32)

time: 82.9 us -> 81.3 us (0.981)
  Pallas kernels: 82.7 us -> 81.1 us
    pallas_call x1, Pallas kernels: 80.3 us -> 78.8 us  [shards(): pl.pallas_call(kernel, out_shape=jax.ShapeDtypeStruct((2, 32, COLS, D), B...]
where the time goes in v6:
time: 81.3 us; the launch traced here: 81.2 us
  Pallas kernels  81.1 us (100%)
    pallas_call x1, Pallas kernels, shards(): pl.pallas_call(kernel, out_shape=jax.ShapeDtypeStruct((2, 32, COLS, D), B...  78.8 us
    pallas_call x1, Pallas kernels, shards(): pl.pallas_call(copy_kernel, out_shape=jax.ShapeDtypeStruct(result.shape,...  2.39 us

profile of v6, /device:TPU:1, one launch (start us, length us, event | category | flops | bytes accessed | tf_op | source)
XLA Modules:
  0.0 81.2 jit_solution(11128017068770106201)
XLA Ops:
  0.0 78.8 %shard_map.127 = bf16[2,32,64,256]{3,2,1,0:T(8,128)(2,1)} custom-call(bf16[64,64,256]{2,1,0:T(8,128)(2,1)} %tokens_hbm.1, f32[1,256]{1,0:T(1,128)} %bitcast.5, bf16[256,1024]{1,0:T(8,128)(2,1)} %w_expand_hbm.1, f32[3,3,1024]{2,1,0:T(4,128)} %dw_kernel_hbm.1, bf16[1024,256]{1,0:T(8,128)(2,1)} %w_project_hbm.1, f32[1,256]{1,0:T(1,128)} %bitcast.6, ...), custom_call_target="tpu_custom_call" | custom-call | tf_op jit(solution)/shard_map/pallas_call | solution.py:575
  78.8 2.4 %shard_map.128 = bf16[64,64,256]{2,1,0:T(8,128)(2,1)} custom-call(bf16[64,64,256]{2,1,0:T(8,128)(2,1)} %bitcast.4), custom_call_target="tpu_custom_call" | custom-call | tf_op jit(solution)/shard_map/pallas_call | solution.py:618

commit v7 on v5

--- a/solution.py
+++ b/solution.py
@@ -52,9 +52,10 @@
 
 
 def head_top(pairs, select):
-    wide = [jnp.maximum(x, pltpu.roll(x, 64, 1)) for x in pairs]
-    lane = lax.broadcasted_iota(jnp.int32, wide[0].shape, 1)
-    top = jnp.where(lane < 64, wide[0], wide[1])
+    lane = lax.broadcasted_iota(jnp.int32, pairs[0].shape, 1)
+    here = jnp.where(lane < 64, pairs[0], pairs[1])
+    there = jnp.where(lane < 64, pairs[1], pairs[0])
+    top = jnp.maximum(here, pltpu.roll(there, 64, 1))
     for shift in (8, 4, 2, 1):
         top = jnp.maximum(top, pltpu.roll(top, 128 - shift, 1))
     high = top.astype(BF16)
@@ -218,9 +219,12 @@
         pltpu.make_async_copy(src, dst, fetch_sem.at[i])
         for i, (src, dst) in enumerate(
             [
-                (tokens_hbm, tokens),
                 (w_expand_hbm, w_expand),
                 (gain_conv_hbm, gain_conv),
+                *[
+                    (tokens_hbm.at[pl.ds(16 * k, 16)], tokens.at[pl.ds(16 * k, 16)])
+                    for k in range(4)
+                ],
                 (dw_kernel_hbm, dw_kernel),
                 (bias_in_block_hbm, bias_in_block),
                 (bias_in_grid_hbm, bias_in_grid),
@@ -243,7 +247,7 @@
         pl.semaphore_signal(barrier, inc=1, device_id=partner(i), device_id_type=MESH)
         return carry
 
-    lax.fori_loop(0, 32, greet, 0)
+    lax.fori_loop(0, 32, greet, 0, unroll=True)
     for side in (west, east):
         pl.semaphore_signal(
             barrier, inc=1, device_id={"lat": lat, "lon": side}, device_id_type=MESH
@@ -264,22 +268,23 @@
             )
 
     average[...] = jnp.full((D, D), 1.0 / D, BF16)
+    def expand_rows(first, count):
+        def store(c, v):
+            e_mid[pl.ds(first + 1, count), :, c : c + 256] = v.reshape(count, COLS, 256)
+
+        x = tokens[pl.ds(first, count)].reshape(count * COLS, D)
+        expand(x, gain_conv[...], average[...], w_expand, store)
+
     for copy in fetched[:3]:
+        copy.wait()
+    expand_rows(0, 8)
+    for copy in fetched[3:6]:
         copy.wait()
     for side in range(2):
         first = pick((16, 256), lambda r, c: c == r * 16 + 15 * side)
         for q in range(4):
             x = tokens[16 * q : 16 * q + 16, 48 * side : 48 * side + 16].reshape(256, D)
             edge[side, 16 * q : 16 * q + 16] = dot(first, x).astype(BF16)
-
-    def expand_rows(first, count):
-        def store(c, v):
-            e_mid[pl.ds(first + 1, count), :, c : c + 256] = v.reshape(count, COLS, 256)
-
-        x = tokens[pl.ds(first, count)].reshape(count * COLS, D)
-        expand(x, gain_conv[...], average[...], w_expand, store)
-
-    expand_rows(0, 9)
 
     inner = jnp.minimum(lat, 1) + jnp.minimum(lats - 1 - lat, 1)
     pl.semaphore_wait(barrier, 34 + 3 * inner)
@@ -331,8 +336,10 @@
         halo_col[0, 80:96] = jnp.zeros((16, D), BF16)
         halo_col[1, 80:96] = jnp.zeros((16, D), BF16)
 
-    expand_rows(31, 10)
-    for copy in fetched[3:]:
+    expand_rows(8, 9)
+    expand_rows(31, 9)
+    expand_rows(40, 9)
+    for copy in fetched[6:]:
         copy.wait()
     for h in range(4):
         masks[h] = pick((16, 128), lambda r, c: (c >> 5) == h)
@@ -440,28 +447,25 @@
 
         lax.fori_loop(0, 32, one, 0, unroll=True)
 
-    def send_back(phase):
-        def one(i, carry):
+    def send_back(phase, q):
+        for j in range(8):
             pltpu.make_async_remote_copy(
-                src_ref=outgoing.at[phase, i // 8, :, lax.rem(i, 8)],
+                src_ref=outgoing.at[phase, q, :, j],
                 dst_ref=out.at[
                     :, phase * 8 + my_row, pl.ds(pl.multiple_of(my_col * 16, 16), 16), :
                 ],
                 send_sem=back_send.at[phase],
                 recv_sem=back_recv.at[phase],
-                device_id=partner(i),
+                device_id={"lat": q, "lon": 4 * j + far},
                 device_id_type=MESH,
             ).start()
-            return carry
-
-        lax.fori_loop(0, 32, one, 0, unroll=True)
 
     def conv_and_block(phase):
         def half(i, carry):
             band = i * 4 + phase
             first = band * 8
 
-            @pl.when((phase > 0) & (band < 7))
+            @pl.when((phase > 1) & (band < 7))
             def _():
                 expand_rows(first + 1, 8)
 
@@ -500,6 +504,7 @@
                 [done[64 * p + 16 * q : 64 * p + 16 * q + 16] for p in range(16)], axis=0
             )
             outgoing[phase, q] = dot(perm[...], x).astype(BF16).reshape(2, 8, 16, D)
+            send_back(phase, q)
 
     def wait_all(ref, sem):
         pltpu.make_async_copy(ref, ref, sem).wait()
@@ -513,7 +518,6 @@
         def _():
             wait_all(received.at[phase - 1], recv_sem.at[phase - 1])
             grid(phase - 1)
-            send_back(phase - 1)
 
         return carry
 
@@ -611,7 +615,7 @@
             pltpu.SemaphoreType.DMA((PHASES,)),
             pltpu.SemaphoreType.DMA((PHASES,)),
             *[pltpu.VMEM(a.shape, a.dtype) for a in operands],
-            pltpu.SemaphoreType.DMA((len(operands),)),
+            pltpu.SemaphoreType.DMA((len(operands) + 3,)),
         ],
         compiler_params=pltpu.CompilerParams(
             collective_id=0, has_side_effects=True, vmem_limit_bytes=60 * 1024 * 1024

time: 82.9 us -> 82.2 us (level)
  no operation moved by 1% of the time
where the time goes in v7:
time: 82.2 us; the launch traced here: 82.1 us
  Pallas kernels  82.1 us (100%)
    pallas_call x1, Pallas kernels, shards(): pl.pallas_call(kernel, out_shape=jax.ShapeDtypeStruct((2, 32, COLS, D), B...  79.7 us
    pallas_call x1, Pallas kernels, shards(): pl.pallas_call(copy_kernel, out_shape=jax.ShapeDtypeStruct(result.shape,...  2.39 us

profile of v7, /device:TPU:1, one launch (start us, length us, event | category | flops | bytes accessed | tf_op | source)
XLA Modules:
  0.0 82.1 jit_solution(4834073155723888829)
XLA Ops:
  0.0 79.7 %shard_map.127 = bf16[2,32,64,256]{3,2,1,0:T(8,128)(2,1)} custom-call(bf16[64,64,256]{2,1,0:T(8,128)(2,1)} %tokens_hbm.1, f32[1,256]{1,0:T(1,128)} %bitcast.5, bf16[256,1024]{1,0:T(8,128)(2,1)} %w_expand_hbm.1, f32[3,3,1024]{2,1,0:T(4,128)} %dw_kernel_hbm.1, bf16[1024,256]{1,0:T(8,128)(2,1)} %w_project_hbm.1, f32[1,256]{1,0:T(1,128)} %bitcast.6, ...), custom_call_target="tpu_custom_call" | custom-call | tf_op jit(solution)/shard_map/pallas_call | solution.py:582
  79.7 2.4 %shard_map.128 = bf16[64,64,256]{2,1,0:T(8,128)(2,1)} custom-call(bf16[64,64,256]{2,1,0:T(8,128)(2,1)} %bitcast.4), custom_call_target="tpu_custom_call" | custom-call | tf_op jit(solution)/shard_map/pallas_call | solution.py:625

commit v8 on v6

--- a/solution.py
+++ b/solution.py
@@ -1,3 +1,5 @@
+import functools
+
 import jax
 import jax.numpy as jnp
 from jax import lax
@@ -11,7 +13,7 @@
 ROWS, COLS, D, HID, HEADS = 64, 64, 256, 1024, 8
 PHASES = 4
 EARLY = 5
-BATCH = 16
+STEPS = 15
 LOG2E = 1.4426950408889634
 
 
@@ -52,15 +54,18 @@
     )
 
 
-def head_top(pairs, select):
-    wide = [jnp.maximum(x, pltpu.roll(x, 64, 1)) for x in pairs]
-    lane = lax.broadcasted_iota(jnp.int32, wide[0].shape, 1)
-    top = jnp.where(lane < 64, wide[0], wide[1])
-    for shift in (8, 4, 2, 1):
-        top = jnp.maximum(top, pltpu.roll(top, 128 - shift, 1))
-    high = top.astype(BF16)
-    low = (top - high.astype(F32)).astype(BF16)
-    return dot(jnp.concatenate([high, low], axis=1), select[...])
+def beside(steps, others):
+    marks = list(steps_count(len(others)))
+    for at, _ in enumerate(steps):
+        while marks and marks[0] <= at:
+            marks.pop(0)
+            others.pop(0)()
+    for other in others:
+        other()
+
+
+def steps_count(count):
+    return (k * STEPS // count for k in range(count))
 
 
 def attend(x_ref, gain, average, w_qkv, bias, w_out, masks, select, ones_bd, qkv, mixed):
@@ -69,52 +74,77 @@
     qkv[:, 0:256] = (dot(n, w_qkv[:, 0:256]) * scale).astype(BF16)
     qkv[:, 256:512] = dot(n, w_qkv[:, 256:512]).astype(BF16)
     qkv[:, 512:768] = dot(n, w_qkv[:, 512:768]).astype(BF16)
-    size = min(BATCH * 64, x_ref.shape[0])
-
-    def batch(first):
-        rows = [pl.ds(first + i * 64, 64) for i in range(size // 64)]
-        scores = [
+    groups = x_ref.shape[0] // 64
+    scores, weights, sums, totals = {}, {}, {}, {}
+
+    def rows(g):
+        return pl.ds(64 * g, 64)
+
+    def score(g):
+        scores[g] = [
+            dot_nt(
+                qkv[rows(g), 128 * u : 128 * u + 128],
+                blocks(qkv[rows(g), 256 + 128 * u : 384 + 128 * u], masks),
+            )
+            + bias[:, 256 * u : 256 * u + 256]
+            for u in range(2)
+        ]
+
+    def soften(batch):
+        pairs = [
             jnp.concatenate(
-                [
-                    dot_nt(
-                        qkv[r, 128 * u : 128 * u + 128],
-                        blocks(qkv[r, 256 + 128 * u : 384 + 128 * u], masks),
-                    )
-                    + bias[:, 256 * u : 256 * u + 256]
-                    for r in rows
-                ],
+                [jnp.maximum(scores[g][u][:, 0:128], scores[g][u][:, 128:256]) for g in batch],
                 axis=0,
             )
             for u in range(2)
         ]
-        top = head_top([jnp.maximum(s[:, 0:128], s[:, 128:256]) for s in scores], select)
-        weights, sums = [], []
-        for u, s in enumerate(scores):
-            t = top[:, 128 * u : 128 * u + 128]
-            a, b = exp2(s[:, 0:128] - t), exp2(s[:, 128:256] - t)
-            sums.append((a + b).astype(BF16))
-            weights.append(jnp.concatenate([a.astype(BF16), b.astype(BF16)], axis=1))
-        total = dot(jnp.concatenate(sums, axis=1), ones_bd[...])
-        values = jnp.concatenate(
+        yield
+        lane = lax.broadcasted_iota(jnp.int32, pairs[0].shape, 1)
+        here = jnp.where(lane < 64, pairs[0], pairs[1])
+        there = jnp.where(lane < 64, pairs[1], pairs[0])
+        top = jnp.maximum(here, pltpu.roll(there, 64, 1))
+        yield
+        for shift in (8, 4, 2, 1):
+            top = jnp.maximum(top, pltpu.roll(top, 128 - shift, 1))
+            yield
+        high = top.astype(BF16)
+        low = (top - high.astype(F32)).astype(BF16)
+        top = dot(jnp.concatenate([high, low], axis=1), select[...])
+        yield
+        for k, g in enumerate(batch):
+            parts, weights[g] = [], []
+            for u, s in enumerate(scores[g]):
+                t = top[64 * k : 64 * k + 64, 128 * u : 128 * u + 128]
+                a, b = exp2(s[:, 0:128] - t), exp2(s[:, 128:256] - t)
+                parts.append((a + b).astype(BF16))
+                weights[g].append(jnp.concatenate([a.astype(BF16), b.astype(BF16)], axis=1))
+            sums[g] = jnp.concatenate(parts, axis=1)
+            yield
+
+    def combine(batch):
+        total = dot(jnp.concatenate([sums[g] for g in batch], axis=0), ones_bd[...])
+        for k, g in enumerate(batch):
+            totals[g] = total[64 * k : 64 * k + 64]
+
+    def value(g):
+        out = jnp.concatenate(
             [
-                jnp.concatenate(
-                    [
-                        dot(
-                            w[64 * k : 64 * k + 64],
-                            blocks(qkv[r, 512 + 128 * u : 640 + 128 * u], masks),
-                        )
-                        for k, r in enumerate(rows)
-                    ],
-                    axis=0,
-                )
-                for u, w in enumerate(weights)
+                dot(w, blocks(qkv[rows(g), 512 + 128 * u : 640 + 128 * u], masks))
+                for u, w in enumerate(weights[g])
             ],
             axis=1,
         )
-        mixed[pl.ds(first, size), :] = (values / total).astype(BF16)
-
-    for first in range(0, x_ref.shape[0], size):
-        batch(first)
+        mixed[rows(g), :] = (out / totals[g]).astype(BF16)
+
+    early, late = range(groups // 2), range(groups // 2, groups)
+    for g in early:
+        score(g)
+    beside(soften(early), [functools.partial(score, g) for g in late])
+    combine(early)
+    beside(soften(late), [functools.partial(value, g) for g in early])
+    combine(late)
+    for g in late:
+        value(g)
     return dot(mixed[...], w_out[...])
 
 
@@ -429,13 +459,13 @@
             [x[64 * b + 8 * a : 64 * b + 8 * a + 8] for a in range(8) for b in range(8)], axis=0
         )
 
-    def send(phase, half):
+    def send(phase):
         def one(i, carry):
             pltpu.make_async_remote_copy(
                 src_ref=blocked.at[
-                    half, phase * 8 + i // 4, pl.ds(pl.multiple_of(lax.rem(i, 4) * 16, 16), 16), :
+                    :, phase * 8 + i // 4, pl.ds(pl.multiple_of(lax.rem(i, 4) * 16, 16), 16), :
                 ],
-                dst_ref=received.at[phase, lat, half, place],
+                dst_ref=received.at[phase, lat, :, place],
                 send_sem=send_sem.at[phase],
                 recv_sem=recv_sem.at[phase],
                 device_id=partner(i),
@@ -468,19 +498,21 @@
 
             conv_band(band)
             x = tokens[pl.ds(first, 8)].reshape(512, D).astype(F32)
-            x = pieces(x + dot(conv[0:512, :], w_project[...])).astype(BF16)
-            mixed[0:512, :] = x
-            result = attend(
-                mixed.at[0:512], gain_block, average, qkv_block, bias_block, out_block, masks, select,
-                ones_bd, qkv.at[0:512], att.at[0:512],
+            rows = pl.ds(pl.multiple_of(i * 512, 512), 512)
+            mixed[rows, :] = pieces(x + dot(conv[0:512, :], w_project[...])).astype(BF16)
+            return carry
+
+        lax.fori_loop(0, 2, half, 0)
+        result = attend(
+            mixed, gain_block, average, qkv_block, bias_block, out_block, masks, select, ones_bd,
+            qkv, att,
+        )
+        result = result + mixed[...].astype(F32)
+        for i in range(2):
+            blocked[i, pl.ds(phase * 8, 8)] = (
+                pieces(result[512 * i : 512 * i + 512]).astype(BF16).reshape(8, 64, D)
             )
-            blocked[i, pl.ds(phase * 8, 8)] = (
-                pieces(result + x.astype(F32)).astype(BF16).reshape(8, 64, D)
-            )
-            send(phase, i)
-            return carry
-
-        lax.fori_loop(0, 2, half, 0)
+        send(phase)
 
     def grid(phase):
         for q in range(4):

time: 81.3 us -> 79.6 us (0.979)
  Pallas kernels: 81.1 us -> 79.5 us
    pallas_call x1, Pallas kernels: 78.8 us -> 77.1 us  [shards(): pl.pallas_call(kernel, out_shape=jax.ShapeDtypeStruct((2, 32, COLS, D), B...]
where the time goes in v8:
time: 79.6 us; the launch traced here: 79.5 us
  Pallas kernels  79.5 us (100%)
    pallas_call x1, Pallas kernels, shards(): pl.pallas_call(kernel, out_shape=jax.ShapeDtypeStruct((2, 32, COLS, D), B...  77.1 us
    pallas_call x1, Pallas kernels, shards(): pl.pallas_call(copy_kernel, out_shape=jax.ShapeDtypeStruct(result.shape,...  2.39 us

profile of v8, /device:TPU:1, one launch (start us, length us, event | category | flops | bytes accessed | tf_op | source)
XLA Modules:
  0.0 79.5 jit_solution(8290659019912993488)
XLA Ops:
  0.0 77.1 %shard_map.127 = bf16[2,32,64,256]{3,2,1,0:T(8,128)(2,1)} custom-call(bf16[64,64,256]{2,1,0:T(8,128)(2,1)} %tokens_hbm.1, f32[1,256]{1,0:T(1,128)} %bitcast.5, bf16[256,1024]{1,0:T(8,128)(2,1)} %w_expand_hbm.1, f32[3,3,1024]{2,1,0:T(4,128)} %dw_kernel_hbm.1, bf16[1024,256]{1,0:T(8,128)(2,1)} %w_project_hbm.1, f32[1,256]{1,0:T(1,128)} %bitcast.6, ...), custom_call_target="tpu_custom_call" | custom-call | tf_op jit(solution)/shard_map/pallas_call | solution.py:607
  77.1 2.4 %shard_map.128 = bf16[64,64,256]{2,1,0:T(8,128)(2,1)} custom-call(bf16[64,64,256]{2,1,0:T(8,128)(2,1)} %bitcast.4), custom_call_target="tpu_custom_call" | custom-call | tf_op jit(solution)/shard_map/pallas_call | solution.py:650

commit v9 on v8

--- a/solution.py
+++ b/solution.py
@@ -12,7 +12,6 @@
 F32 = jnp.float32
 ROWS, COLS, D, HID, HEADS = 64, 64, 256, 1024, 8
 PHASES = 4
-EARLY = 5
 STEPS = 15
 LOG2E = 1.4426950408889634
 
@@ -249,9 +248,12 @@
         pltpu.make_async_copy(src, dst, fetch_sem.at[i])
         for i, (src, dst) in enumerate(
             [
-                (tokens_hbm, tokens),
                 (w_expand_hbm, w_expand),
                 (gain_conv_hbm, gain_conv),
+                *[
+                    (tokens_hbm.at[pl.ds(16 * k, 16)], tokens.at[pl.ds(16 * k, 16)])
+                    for k in range(4)
+                ],
                 (dw_kernel_hbm, dw_kernel),
                 (bias_in_block_hbm, bias_in_block),
                 (bias_in_grid_hbm, bias_in_grid),
@@ -295,26 +297,23 @@
             )
 
     average[...] = jnp.full((D, D), 1.0 / D, BF16)
+    def expand_rows(first, count):
+        def store(c, v):
+            e_mid[pl.ds(first + 1, count), :, c : c + 256] = v.reshape(count, COLS, 256)
+
+        x = tokens[pl.ds(first, count)].reshape(count * COLS, D)
+        expand(x, gain_conv[...], average[...], w_expand, store)
+
     for copy in fetched[:3]:
+        copy.wait()
+    expand_rows(0, 8)
+    for copy in fetched[3:6]:
         copy.wait()
     for side in range(2):
         first = pick((16, 256), lambda r, c: c == r * 16 + 15 * side)
         for q in range(4):
             x = tokens[16 * q : 16 * q + 16, 48 * side : 48 * side + 16].reshape(256, D)
             edge[side, 16 * q : 16 * q + 16] = dot(first, x).astype(BF16)
-
-    def expand_rows(first, count):
-        def store(c, v):
-            e_mid[pl.ds(first + 1, count), :, c : c + 256] = v.reshape(count, COLS, 256)
-
-        x = tokens[pl.ds(first, count)].reshape(count * COLS, D)
-        expand(x, gain_conv[...], average[...], w_expand, store)
-
-    def expand_band(band, carry):
-        expand_rows(band * 8, 8)
-        return carry
-
-    lax.fori_loop(0, EARLY, expand_band, 0)
 
     inner = jnp.minimum(lat, 1) + jnp.minimum(lats - 1 - lat, 1)
     pl.semaphore_wait(barrier, 34 + 3 * inner)
@@ -366,8 +365,10 @@
         halo_col[0, 80:96] = jnp.zeros((16, D), BF16)
         halo_col[1, 80:96] = jnp.zeros((16, D), BF16)
 
-    lax.fori_loop(EARLY, 8, expand_band, 0)
-    for copy in fetched[3:]:
+    expand_rows(8, 9)
+    expand_rows(31, 9)
+    expand_rows(40, 9)
+    for copy in fetched[6:]:
         copy.wait()
     for h in range(4):
         masks[h] = pick((16, 128), lambda r, c: (c >> 5) == h)
@@ -475,26 +476,31 @@
 
         lax.fori_loop(0, 32, one, 0, unroll=True)
 
-    def send_back(phase):
-        def one(i, carry):
+    def send_back(phase, q):
+        for j in range(8):
             pltpu.make_async_remote_copy(
-                src_ref=outgoing.at[phase, i // 8, :, lax.rem(i, 8)],
+                src_ref=outgoing.at[phase, q, :, j],
                 dst_ref=out.at[
                     :, phase * 8 + my_row, pl.ds(pl.multiple_of(my_col * 16, 16), 16), :
                 ],
                 send_sem=back_send.at[phase],
                 recv_sem=back_recv.at[phase],
-                device_id=partner(i),
+                device_id={"lat": q, "lon": 4 * j + far},
                 device_id_type=MESH,
             ).start()
-            return carry
-
-        lax.fori_loop(0, 32, one, 0, unroll=True)
 
     def conv_and_block(phase):
         def half(i, carry):
             band = i * 4 + phase
             first = band * 8
+
+            @pl.when((phase > 1) & (band < 7))
+            def _():
+                expand_rows(first + 1, 8)
+
+            @pl.when(band == 7)
+            def _():
+                expand_rows(first + 1, 7)
 
             conv_band(band)
             x = tokens[pl.ds(first, 8)].reshape(512, D).astype(F32)
@@ -529,6 +535,7 @@
                 [done[64 * p + 16 * q : 64 * p + 16 * q + 16] for p in range(16)], axis=0
             )
             outgoing[phase, q] = dot(perm[...], x).astype(BF16).reshape(2, 8, 16, D)
+            send_back(phase, q)
 
     def wait_all(ref, sem):
         pltpu.make_async_copy(ref, ref, sem).wait()
@@ -542,7 +549,6 @@
         def _():
             wait_all(received.at[phase - 1], recv_sem.at[phase - 1])
             grid(phase - 1)
-            send_back(phase - 1)
 
         return carry
 
@@ -640,7 +646,7 @@
             pltpu.SemaphoreType.DMA((PHASES,)),
             pltpu.SemaphoreType.DMA((PHASES,)),
             *[pltpu.VMEM(a.shape, a.dtype) for a in operands],
-            pltpu.SemaphoreType.DMA((len(operands),)),
+            pltpu.SemaphoreType.DMA((len(operands) + 3,)),
         ],
         compiler_params=pltpu.CompilerParams(
             collective_id=0, has_side_effects=True, vmem_limit_bytes=60 * 1024 * 1024

time: 79.6 us -> 82.5 us (1.036)
  Pallas kernels: 79.5 us -> 82.2 us
    pallas_call x1, Pallas kernels: 77.1 us -> 79.8 us  [shards(): pl.pallas_call(kernel, out_shape=jax.ShapeDtypeStruct((2, 32, COLS, D), B...]
where the time goes in v9:
time: 82.5 us; the launch traced here: 82.3 us
  Pallas kernels  82.2 us (100%)
    pallas_call x1, Pallas kernels, shards(): pl.pallas_call(kernel, out_shape=jax.ShapeDtypeStruct((2, 32, COLS, D), B...  79.8 us
    pallas_call x1, Pallas kernels, shards(): pl.pallas_call(copy_kernel, out_shape=jax.ShapeDtypeStruct(result.shape,...  2.39 us

profile of v9, /device:TPU:1, one launch (start us, length us, event | category | flops | bytes accessed | tf_op | source)
XLA Modules:
  0.0 82.3 jit_solution(2891268609770233045)
XLA Ops:
  0.0 79.8 %shard_map.127 = bf16[2,32,64,256]{3,2,1,0:T(8,128)(2,1)} custom-call(bf16[64,64,256]{2,1,0:T(8,128)(2,1)} %tokens_hbm.1, f32[1,256]{1,0:T(1,128)} %bitcast.5, bf16[256,1024]{1,0:T(8,128)(2,1)} %w_expand_hbm.1, f32[3,3,1024]{2,1,0:T(4,128)} %dw_kernel_hbm.1, bf16[1024,256]{1,0:T(8,128)(2,1)} %w_project_hbm.1, f32[1,256]{1,0:T(1,128)} %bitcast.6, ...), custom_call_target="tpu_custom_call" | custom-call | tf_op jit(solution)/shard_map/pallas_call | solution.py:613
  79.8 2.4 %shard_map.128 = bf16[64,64,256]{2,1,0:T(8,128)(2,1)} custom-call(bf16[64,64,256]{2,1,0:T(8,128)(2,1)} %bitcast.4), custom_call_target="tpu_custom_call" | custom-call | tf_op jit(solution)/shard_map/pallas_call | solution.py:656
